TPU v7x, 256 devices: a whole 4x4x8 slice. The times are simulated.
256 devices in a mesh: seq: 32 (over y, x, core), head: 8 (over z).
Axes of the slice: x: 4, y: 4, z: 8, core: 2. Of those that a mesh axis runs over, the one named last changes fastest.
Arguments:
- query_rows: bfloat16 [32768, 4096], P(('seq', 'head')), may hold values from -6 to 6
- key_rows: bfloat16 [32768, 4096], P(('seq', 'head')), may hold values from -6 to 6
- value_rows: bfloat16 [32768, 4096], P(('seq', 'head')), may hold values from -6 to 6
- log_decay: bfloat16 [32768, 4096], P(('seq', 'head')), may hold values from -1 to 0
- write_rate: bfloat16 [32768, 32], P(('seq', 'head')), may hold values from 0.0039 to 0.91
Outputs:
- attended: bfloat16 [32768, 4096], P(('seq', 'head'))
All inputs are finite; a program needn't handle non-finite values.
Results may differ from a plain program's by a relative error of at most 0.0012.
Values may be sent and summed in bfloat16 or wider, within the bound.
A program may use at most 192 MiB of HBM per device.

v0:
```python
import jax
import jax.numpy as jnp
from jax import lax
from jax.sharding import PartitionSpec as P

DK = 128
BLOCK = 64


epsilon = 1e-06
highest = lax.Precision.HIGHEST


def shifted_2(x, axis, by):
    count = lax.axis_size(axis)
    pairs = [(i, i + by) for i in range(count) if 0 <= i + by < count]
    return lax.ppermute(x, axis, pairs)


def unit_rows(matrix):
    return matrix * lax.rsqrt(jnp.sum(matrix * matrix, axis=-1, keepdims=True) + epsilon)


def block_maps(query_blk, key_blk, value_blk, decay_blk, rate_blk):
    length = query_blk.shape[2]
    width = query_blk.shape[3]
    query_unit = unit_rows(query_blk)
    key_unit = unit_rows(key_blk)
    cumulative = jnp.cumsum(decay_blk, axis=2)
    middle = cumulative[:, :, length // 2 : length // 2 + 1, :]
    closing = cumulative[:, :, length - 1 : length, :]
    ahead = key_unit * jnp.exp(cumulative - middle)
    behind = key_unit * jnp.exp(middle - cumulative)
    query_ahead = query_unit * jnp.exp(cumulative - middle)
    positions = jnp.arange(length)
    strict = positions[:, None] > positions[None, :]
    inclusive = positions[:, None] >= positions[None, :]
    weights = rate_blk[:, :, None, :]
    among = (
        jnp.where(strict, jnp.einsum("nhid,nhjd->nhij", ahead, behind, precision=highest), 0.0)
        * weights
    )
    attend = (
        jnp.where(
            inclusive, jnp.einsum("nhid,nhjd->nhij", query_ahead, behind, precision=highest), 0.0
        )
        * weights
    )
    system = jnp.eye(length, dtype=jnp.float32) + among
    key_past = key_unit * jnp.exp(cumulative)
    solved = jax.scipy.linalg.solve_triangular(
        system, jnp.concatenate([value_blk, key_past], axis=-1), lower=True, unit_diagonal=True
    )
    update = solved[..., :width]
    reach = solved[..., width:]
    written = key_unit * jnp.exp(closing - cumulative) * rate_blk[..., None]
    decay_diag = jnp.eye(width, dtype=jnp.float32) * jnp.exp(closing)[:, :, 0, :, None]
    transition = decay_diag - jnp.einsum("nhjd,nhje->nhde", written, reach, precision=highest)
    carried = jnp.einsum("nhjd,nhje->nhde", written, update, precision=highest)
    readout = query_unit * jnp.exp(cumulative) - jnp.einsum(
        "nhij,nhjd->nhid", attend, reach, precision=highest
    )
    local_part = jnp.einsum("nhij,nhjd->nhid", attend, update, precision=highest)
    return (readout, local_part, transition, carried)


def compose(earlier, later):
    moved = jnp.einsum("...de,...ef->...df", later[0], earlier[0], precision=highest)
    shifted = jnp.einsum("...de,...ef->...df", later[0], earlier[1], precision=highest) + later[1]
    return (moved, shifted)


def to_blocks(matrix, heads_here):
    rows = matrix.shape[0]
    return (
        matrix.reshape(rows // BLOCK, BLOCK, heads_here, -1)
        .transpose(0, 2, 1, 3)
        .astype(jnp.float32)
    )


def head_layer(query_rows, key_rows, value_rows, log_decay, write_rate, incoming):
    rows, heads_here = write_rate.shape
    rates = (
        write_rate.reshape(rows // BLOCK, BLOCK, heads_here).transpose(0, 2, 1).astype(jnp.float32)
    )
    readout, local_part, transition, carried = block_maps(
        to_blocks(query_rows, heads_here),
        to_blocks(key_rows, heads_here),
        to_blocks(value_rows, heads_here),
        to_blocks(log_decay, heads_here),
        rates,
    )
    identity_mat = jnp.broadcast_to(jnp.eye(DK, dtype=jnp.float32), transition.shape[1:])
    start_pair = (identity_mat, jnp.zeros_like(identity_mat))

    def gather_pair(pair, pieces):
        return (compose(pair, pieces), None)

    shard_pair, unused = lax.scan(gather_pair, start_pair, (transition, carried))
    entering = incoming(shard_pair)

    def run_state(memory, pieces):
        move_blk, carry_blk, read_blk, local_blk = pieces
        out_blk = local_blk + jnp.einsum("hid,hde->hie", read_blk, memory, precision=highest)
        memory = jnp.einsum("hde,hef->hdf", move_blk, memory, precision=highest) + carry_blk
        return (memory, out_blk)

    final_state, result = lax.scan(run_state, entering, (transition, carried, readout, local_part))
    return result.transpose(0, 2, 1, 3).reshape(rows, heads_here * DK).astype(jnp.bfloat16)


def local(query_rows, key_rows, value_rows, log_decay, write_rate):
    moved = (
        lax.all_to_all(query_rows, "head", split_axis=1, concat_axis=0, tiled=True),
        lax.all_to_all(key_rows, "head", split_axis=1, concat_axis=0, tiled=True),
        lax.all_to_all(value_rows, "head", split_axis=1, concat_axis=0, tiled=True),
        lax.all_to_all(log_decay, "head", split_axis=1, concat_axis=0, tiled=True),
        lax.all_to_all(write_rate, "head", split_axis=1, concat_axis=0, tiled=True),
    )

    def incoming_group(shard_pair):

        def relay_turn(counter, memory):
            leaving = (
                jnp.einsum("hde,hef->hdf", shard_pair[0], memory, precision=highest) + shard_pair[1]
            )
            return shifted_2(leaving, "seq", 1)

        return lax.fori_loop(0, lax.axis_size("seq") - 1, relay_turn, jnp.zeros_like(shard_pair[1]))

    grouped = head_layer(moved[0], moved[1], moved[2], moved[3], moved[4], incoming_group)
    return lax.all_to_all(grouped, "head", split_axis=0, concat_axis=1, tiled=True)


def solution(mesh):
    return jax.shard_map(
        local,
        mesh=mesh,
        in_specs=(
            P(("seq", "head"), None),
            P(("seq", "head"), None),
            P(("seq", "head"), None),
            P(("seq", "head"), None),
            P(("seq", "head"), None),
        ),
        out_specs=P(("seq", "head"), None),
        check_vma=False,
    )
```

profile of v0, /device:TPU:17, one launch (start us, length us, event | category | flops | bytes accessed | tf_op | source)
XLA Modules:
  0.0 940.0 jit_solution(12245375366688922142)
XLA Ops:
  0.0 8.2 all-to-all-start.2
  8.2 2.4 copy.140
  10.6 4.2 all-to-all-done.2
  14.8 3.6 all-to-all-start
  19.4 28.0 %all-to-all-done = bf16[128,8,512]{2,0,1:T(8,128)(2,1)S(1)} async-done(((bf16[128,8,512]{2,0,1:T(8,128)(2,1)}), bf16[128,8,512]{2,0,1:T(8,128)(2,1)S(1)}, u32[]{:S(2)}, u32[]{:S(2)}) %all-to-all-start) | async-done | bytes 1048608 | tf_op jit(solution)/shard_map/all_to_all | solution.py:118
  47.4 3.6 all-to-all-start.1
  53.8 26.4 %all-to-all-done.1 = bf16[128,8,512]{2,0,1:T(8,128)(2,1)S(1)} async-done(((bf16[128,8,512]{2,0,1:T(8,128)(2,1)}), bf16[128,8,512]{2,0,1:T(8,128)(2,1)S(1)}, u32[]{:S(2)}, u32[]{:S(2)}) %all-to-all-start.1) | async-done | bytes 1048608 | tf_op jit(solution)/shard_map/all_to_all | solution.py:116
  80.2 3.6 all-to-all-start.3
  89.0 3.0 convert_bitcast_fusion.2
  93.2 19.6 %all-to-all-done.3 = bf16[128,8,512]{2,0,1:T(8,128)(2,1)S(1)} async-done(((bf16[128,8,512]{2,0,1:T(8,128)(2,1)}), bf16[128,8,512]{2,0,1:T(8,128)(2,1)S(1)}, u32[]{:S(2)}, u32[]{:S(2)}) %all-to-all-start.3) | async-done | bytes 1048608 | tf_op jit(solution)/shard_map/all_to_all | solution.py:117
  112.9 4.2 all-to-all-start.4
  117.8 2.9 reshape.79
  123.1 7.2 add_bitcast_fusion
  130.3 316.0 %custom-call.4 = f32[16,4,1,64,64]{3,4,2,1,0:T(8,128)} custom-call(f32[16,4,1,64,64]{4,3,2,1,0:T(8,128)} %add_bitcast_fusion), custom_call_target="InvertDiagBlocksLowerTriangular" | custom-call | tf_op jit(solution)/shard_map/jit(_solve_triangular)/vmap(vmap())/triangular_solve | solution.py:51
  447.9 3.0 reshape.81
  450.9 3.4 copy.136
  454.3 3.3 exponential_multiply_fusion.1
  457.5 2.8 convert_bitcast_fusion
  460.4 3.0 reshape.82
  465.8 7.7 fusion.28
  473.6 4.2 fusion.19
  477.8 5.5 multiply_subtract_fusion.1
  483.3 3.8 fusion.32
  487.2 10.3 %fusion.34 = f32[16,4,128,128]{3,2,1,0:T(8,128)} fusion(f32[16,4,64,256]{3,2,1,0:T(8,128)S(1)} %fusion.19, f32[16,4,64,128]{3,0,1,2:T(8,128)S(1)} %fusion.26, f32[16,64,4,128]{3,2,1,0:T(4,128)S(1)} %copy-done.2, f32[16,4,64]{2,1,0:T(4,128)S(1)} %copy.64, f32[16,4,128]{2,1,0:T(4,128)S(1)} %copy.61, f32[16,4,64]{2,1,0:T(4,128)S(1)} %add_rsqrt_fusion.1), kind=kOutput, calls=%fused_computation.54 | convolution fusion | flops 807403520 | bytes 10584064 | tf_op jit(solution)/shard_map/nhjd,nhje->nhde/dot_general | solution.py:59
  497.5 10.9 %multiply_subtract_fusion = f32[16,4,128,128]{3,2,1,0:T(8,128)} fusion(f32[16,4,128]{2,1,0:T(4,128)S(1)} %copy.58, f32[128,128]{1,0:T(8,128)S(1)} %copy-done.14, f32[16,4,64,256]{3,2,1,0:T(8,128)S(1)} %fusion.19, f32[16,4,64,128]{3,0,1,2:T(8,128)S(1)} %fusion.26, f32[16,64,4,128]{3,2,1,0:T(4,128)S(1)} %copy-done.2, f32[16,4,64]{2,1,0:T(4,128)S(1)} %copy.64, ...), kind=kOutput, calls=%fused_computation.27 | convolution fusion | flops 809500672 | bytes 10682368 | tf_op jit(solution)/shard_map/nhjd,nhje->nhde/dot_general | solution.py:58
  508.4 45.7 %while.37 = (s32[]{:T(128)}, f32[4,128,128]{2,1,0:T(8,128)S(1)}, f32[4,128,128]{2,1,0:T(8,128)S(1)}, f32[16,4,128,128]{3,2,1,0:T(8,128)}, f32[16,4,128,128]{3,2,1,0:T(8,128)}, /*index=5*/s32[]{:T(128)}, s32[]{:T(128)}) while((s32[]{:T(128)}, f32[4,128,128]{2,1,0:T(8,128)S(1)}, f32[4,128,128]{2,1,0:T(8,128)S(1)}, ...), condition=%wide.region_3.4_spmd.clone, body=%wide.region_2.0_spmd.clone.sunk | while | flops 201457664 | bytes 2885207 | solution.py:100
  554.2 309.9 %while.35 = (s32[]{:T(128)}, f32[4,128,128]{2,1,0:T(8,128)S(1)}, f32[4,128,128]{2,1,0:T(8,128)S(1)}, f32[4,128,128]{2,1,0:T(8,128)S(1)}, s32[]{:T(128)}) while((s32[]{:T(128)}, f32[4,128,128]{2,1,0:T(8,128)S(1)}, f32[4,128,128]{2,1,0:T(8,128)S(1)}, f32[4,128,128]{2,1,0:T(8,128)S(1)}, s32[]{:T(128)}) %tuple.55), condition=%wide.region_5.6_spmd, body=%wide.region_4.5_spmd.sunk | while | flops 100728832 | bytes 2097253 | solution.py:130
  554.6 3.5 collective-permute-start
  558.1 3.3 collective-permute-done
  561.8 4.4 collective-permute-start
  566.2 3.3 collective-permute-done
  569.9 4.4 collective-permute-start
  574.3 4.1 collective-permute-done
  578.9 3.5 collective-permute-start
  582.4 6.2 collective-permute-done
  591.0 7.9 collective-permute-done
  601.2 7.9 collective-permute-done
  611.4 7.9 collective-permute-done
  621.6 7.9 collective-permute-done
  631.8 7.9 collective-permute-done
  642.0 7.9 collective-permute-done
  652.2 7.9 collective-permute-done
  662.4 7.9 collective-permute-done
  672.6 7.9 collective-permute-done
  682.8 7.9 collective-permute-done
  693.0 7.9 collective-permute-done
  703.2 7.9 collective-permute-done
  713.4 7.9 collective-permute-done
  723.6 7.9 collective-permute-done
  733.8 7.9 collective-permute-done
  744.0 7.9 collective-permute-done
  754.2 7.9 collective-permute-done
  764.4 7.9 collective-permute-done
  774.6 7.9 collective-permute-done
  784.8 7.9 collective-permute-done
  795.0 7.9 collective-permute-done
  805.2 7.9 collective-permute-done
  815.4 7.9 collective-permute-done
  825.6 7.9 collective-permute-done
  835.8 7.9 collective-permute-done
  846.0 7.9 collective-permute-done
  856.2 7.9 collective-permute-done
  864.1 45.2 %while.36 = (s32[]{:T(128)}, f32[4,128,128]{2,1,0:T(8,128)S(1)}, bf16[16,4,64,128]{3,2,1,0:T(8,128)(2,1)S(1)}, f32[16,4,128,128]{3,2,1,0:T(8,128)}, f32[16,4,128...) while((s32[]{:T(128)}, f32[4,128,128]{2,1,0:T(8,128)S(1)}, ...), condition=%wide.region_8.9_spmd, body=%wide.region_7.8_spmd.sunk | while | flops 151093248 | bytes 2230357 | solution.py:109
  910.6 27.5 %all_to_all.81 = bf16[8,128,512]{2,1,0:T(8,128)(2,1)S(1)} all-to-all(bf16[8,128,512]{2,1,0:T(8,128)(2,1)S(1)} %convert_element_type.111), channel_id=1, replica_groups=mesh['seq'=32,'head'=8] {'head'}, dimensions={0} | all-to-all | bytes 2097152 | tf_op jit(solution)/shard_map/all_to_all | solution.py:133
  (241 shorter events, 174.4 us)
Async XLA Ops:
  0.0 14.8 %all-to-all-start.2 = ((bf16[128,8,4]{0,2,1:T(4,128)(2,1)}), bf16[128,8,4]{0,2,1:T(4,128)(2,1)S(1)}, u32[]{:S(2)}, u32[]{:S(2)}) async-start(bf16[128,8,4]{0,2,1:T(4,128)(2,1)} %bitcast.147), calls=%async_computation.2 | async-start | bytes 16384 | tf_op jit(solution)/shard_map/all_to_all | solution.py:119
  8.2 10.1 %copy-start.10 = (bf16[128,4096]{1,0:T(8,128)(2,1)S(1)}, bf16[128,4096]{1,0:T(8,128)(2,1)}, u32[]{:S(2)}) copy-start(bf16[128,4096]{1,0:T(8,128)(2,1)} %param.12) | copy-start | bytes 3145732
  14.8 32.7 %all-to-all-start = ((bf16[128,8,512]{2,0,1:T(8,128)(2,1)}), bf16[128,8,512]{2,0,1:T(8,128)(2,1)S(1)}, u32[]{:S(2)}, u32[]{:S(2)}) async-start(bf16[128,8,512]{2,0,1:T(8,128)(2,1)} %bitcast.108), calls=%async_computation | async-start | bytes 2097152 | tf_op jit(solution)/shard_map/all_to_all | solution.py:118
  18.3 32.7 %copy-start.11 = (bf16[128,4096]{1,0:T(8,128)(2,1)S(1)}, bf16[128,4096]{1,0:T(8,128)(2,1)}, u32[]{:S(2)}) copy-start(bf16[128,4096]{1,0:T(8,128)(2,1)} %param.13) | copy-start | bytes 3145732
  47.4 4.7 copy-start.7
  47.4 32.7 %all-to-all-start.1 = ((bf16[128,8,512]{2,0,1:T(8,128)(2,1)}), bf16[128,8,512]{2,0,1:T(8,128)(2,1)S(1)}, u32[]{:S(2)}, u32[]{:S(2)}) async-start(bf16[128,8,512]{2,0,1:T(8,128)(2,1)} %bitcast.107), calls=%async_computation.1 | async-start | bytes 2097152 | tf_op jit(solution)/shard_map/all_to_all | solution.py:116
  51.0 1.6 copy-start.12
  80.2 5.6 copy-start.8
  80.2 32.7 %all-to-all-start.3 = ((bf16[128,8,512]{2,0,1:T(8,128)(2,1)}), bf16[128,8,512]{2,0,1:T(8,128)(2,1)S(1)}, u32[]{:S(2)}, u32[]{:S(2)}) async-start(bf16[128,8,512]{2,0,1:T(8,128)(2,1)} %bitcast.138), calls=%async_computation.3 | async-start | bytes 2097152 | tf_op jit(solution)/shard_map/all_to_all | solution.py:117
  89.0 3.0 copy-start.6
  112.9 344.7 %all-to-all-start.4 = ((bf16[128,8,512]{2,0,1:T(8,128)(2,1)}), bf16[128,8,512]{2,0,1:T(8,128)(2,1)}, u32[]{:S(2)}, u32[]{:S(2)}) async-start(bf16[128,8,512]{2,0,1:T(8,128)(2,1)} %bitcast.137), calls=%async_computation.4 | async-start | bytes 2097152 | tf_op jit(solution)/shard_map/all_to_all | solution.py:115
  120.7 2.4 copy-start
  120.7 2.4 copy-start.15
  120.7 2.4 copy-start.18
  450.8 3.4 copy-start.1
  463.3 2.4 copy-start.2
  465.7 7.8 copy-start.4
  465.8 7.8 copy-start.5
  465.8 7.8 copy-start.9
  473.6 4.3 copy-start.3
  483.3 3.8 copy-start.17
  483.3 3.9 copy-start.16
  487.2 10.3 %copy-start.14 = (f32[128,128]{1,0:T(8,128)S(1)}, f32[128,128]{1,0:T(8,128)}, u32[]{:S(2)}) copy-start(f32[128,128]{1,0:T(8,128)} %fusion.57) | copy-start | bytes 196612
  554.2 309.9 %copy-start.13 = (bf16[16,4,64,128]{3,2,1,0:T(8,128)(2,1)S(1)}, bf16[16,4,64,128]{3,2,1,0:T(8,128)(2,1)}, u32[]{:S(2)}) copy-start(bf16[16,4,64,128]{3,2,1,0:T(8,128)(2,1)} %custom-call.6) | copy-start | bytes 3145732
  554.6 6.8 collective-permute-start
  561.8 7.7 collective-permute-start
  569.9 8.5 collective-permute-start
  578.9 9.8 %collective-permute-start = (f32[4,128,128]{2,1,0:T(8,128)S(1)}, f32[4,128,128]{2,1,0:T(8,128)S(1)}, u32[]{:S(2)}, u32[]{:S(2)}) collective-permute-start(f32[4,128,128]{2,1,0:T(8,128)S(1)} %convolution_add_fusion.7), channel_id=1, source_target_pairs={{0,8},{8,16},{16,24},{24,32},{32,40},{40,48},{48,56},{56,64},{64,7... | collective-permute-start | bytes 786440 | tf_op jit(solution)/shard_map/while/body/eval_jaxpr/ppermute | solution.py:17
  589.1 9.8 %collective-permute-start = (f32[4,128,128]{2,1,0:T(8,128)S(1)}, f32[4,128,128]{2,1,0:T(8,128)S(1)}, u32[]{:S(2)}, u32[]{:S(2)}) collective-permute-start(f32[4,128,128]{2,1,0:T(8,128)S(1)} %convolution_add_fusion.7), channel_id=1, source_target_pairs={{0,8},{8,16},{16,24},{24,32},{32,40},{40,48},{48,56},{56,64},{64,7... | collective-permute-start | bytes 786440 | tf_op jit(solution)/shard_map/while/body/eval_jaxpr/ppermute | solution.py:17
  599.3 9.8 %collective-permute-start = (f32[4,128,128]{2,1,0:T(8,128)S(1)}, f32[4,128,128]{2,1,0:T(8,128)S(1)}, u32[]{:S(2)}, u32[]{:S(2)}) collective-permute-start(f32[4,128,128]{2,1,0:T(8,128)S(1)} %convolution_add_fusion.7), channel_id=1, source_target_pairs={{0,8},{8,16},{16,24},{24,32},{32,40},{40,48},{48,56},{56,64},{64,7... | collective-permute-start | bytes 786440 | tf_op jit(solution)/shard_map/while/body/eval_jaxpr/ppermute | solution.py:17
  609.5 9.8 %collective-permute-start = (f32[4,128,128]{2,1,0:T(8,128)S(1)}, f32[4,128,128]{2,1,0:T(8,128)S(1)}, u32[]{:S(2)}, u32[]{:S(2)}) collective-permute-start(f32[4,128,128]{2,1,0:T(8,128)S(1)} %convolution_add_fusion.7), channel_id=1, source_target_pairs={{0,8},{8,16},{16,24},{24,32},{32,40},{40,48},{48,56},{56,64},{64,7... | collective-permute-start | bytes 786440 | tf_op jit(solution)/shard_map/while/body/eval_jaxpr/ppermute | solution.py:17
  619.7 9.8 %collective-permute-start = (f32[4,128,128]{2,1,0:T(8,128)S(1)}, f32[4,128,128]{2,1,0:T(8,128)S(1)}, u32[]{:S(2)}, u32[]{:S(2)}) collective-permute-start(f32[4,128,128]{2,1,0:T(8,128)S(1)} %convolution_add_fusion.7), channel_id=1, source_target_pairs={{0,8},{8,16},{16,24},{24,32},{32,40},{40,48},{48,56},{56,64},{64,7... | collective-permute-start | bytes 786440 | tf_op jit(solution)/shard_map/while/body/eval_jaxpr/ppermute | solution.py:17
  629.9 9.8 %collective-permute-start = (f32[4,128,128]{2,1,0:T(8,128)S(1)}, f32[4,128,128]{2,1,0:T(8,128)S(1)}, u32[]{:S(2)}, u32[]{:S(2)}) collective-permute-start(f32[4,128,128]{2,1,0:T(8,128)S(1)} %convolution_add_fusion.7), channel_id=1, source_target_pairs={{0,8},{8,16},{16,24},{24,32},{32,40},{40,48},{48,56},{56,64},{64,7... | collective-permute-start | bytes 786440 | tf_op jit(solution)/shard_map/while/body/eval_jaxpr/ppermute | solution.py:17
  640.1 9.8 %collective-permute-start = (f32[4,128,128]{2,1,0:T(8,128)S(1)}, f32[4,128,128]{2,1,0:T(8,128)S(1)}, u32[]{:S(2)}, u32[]{:S(2)}) collective-permute-start(f32[4,128,128]{2,1,0:T(8,128)S(1)} %convolution_add_fusion.7), channel_id=1, source_target_pairs={{0,8},{8,16},{16,24},{24,32},{32,40},{40,48},{48,56},{56,64},{64,7... | collective-permute-start | bytes 786440 | tf_op jit(solution)/shard_map/while/body/eval_jaxpr/ppermute | solution.py:17
  650.3 9.8 %collective-permute-start = (f32[4,128,128]{2,1,0:T(8,128)S(1)}, f32[4,128,128]{2,1,0:T(8,128)S(1)}, u32[]{:S(2)}, u32[]{:S(2)}) collective-permute-start(f32[4,128,128]{2,1,0:T(8,128)S(1)} %convolution_add_fusion.7), channel_id=1, source_target_pairs={{0,8},{8,16},{16,24},{24,32},{32,40},{40,48},{48,56},{56,64},{64,7... | collective-permute-start | bytes 786440 | tf_op jit(solution)/shard_map/while/body/eval_jaxpr/ppermute | solution.py:17
  660.5 9.8 %collective-permute-start = (f32[4,128,128]{2,1,0:T(8,128)S(1)}, f32[4,128,128]{2,1,0:T(8,128)S(1)}, u32[]{:S(2)}, u32[]{:S(2)}) collective-permute-start(f32[4,128,128]{2,1,0:T(8,128)S(1)} %convolution_add_fusion.7), channel_id=1, source_target_pairs={{0,8},{8,16},{16,24},{24,32},{32,40},{40,48},{48,56},{56,64},{64,7... | collective-permute-start | bytes 786440 | tf_op jit(solution)/shard_map/while/body/eval_jaxpr/ppermute | solution.py:17
  670.7 9.8 %collective-permute-start = (f32[4,128,128]{2,1,0:T(8,128)S(1)}, f32[4,128,128]{2,1,0:T(8,128)S(1)}, u32[]{:S(2)}, u32[]{:S(2)}) collective-permute-start(f32[4,128,128]{2,1,0:T(8,128)S(1)} %convolution_add_fusion.7), channel_id=1, source_target_pairs={{0,8},{8,16},{16,24},{24,32},{32,40},{40,48},{48,56},{56,64},{64,7... | collective-permute-start | bytes 786440 | tf_op jit(solution)/shard_map/while/body/eval_jaxpr/ppermute | solution.py:17
  680.9 9.8 %collective-permute-start = (f32[4,128,128]{2,1,0:T(8,128)S(1)}, f32[4,128,128]{2,1,0:T(8,128)S(1)}, u32[]{:S(2)}, u32[]{:S(2)}) collective-permute-start(f32[4,128,128]{2,1,0:T(8,128)S(1)} %convolution_add_fusion.7), channel_id=1, source_target_pairs={{0,8},{8,16},{16,24},{24,32},{32,40},{40,48},{48,56},{56,64},{64,7... | collective-permute-start | bytes 786440 | tf_op jit(solution)/shard_map/while/body/eval_jaxpr/ppermute | solution.py:17
  691.1 9.8 %collective-permute-start = (f32[4,128,128]{2,1,0:T(8,128)S(1)}, f32[4,128,128]{2,1,0:T(8,128)S(1)}, u32[]{:S(2)}, u32[]{:S(2)}) collective-permute-start(f32[4,128,128]{2,1,0:T(8,128)S(1)} %convolution_add_fusion.7), channel_id=1, source_target_pairs={{0,8},{8,16},{16,24},{24,32},{32,40},{40,48},{48,56},{56,64},{64,7... | collective-permute-start | bytes 786440 | tf_op jit(solution)/shard_map/while/body/eval_jaxpr/ppermute | solution.py:17
  701.3 9.8 %collective-permute-start = (f32[4,128,128]{2,1,0:T(8,128)S(1)}, f32[4,128,128]{2,1,0:T(8,128)S(1)}, u32[]{:S(2)}, u32[]{:S(2)}) collective-permute-start(f32[4,128,128]{2,1,0:T(8,128)S(1)} %convolution_add_fusion.7), channel_id=1, source_target_pairs={{0,8},{8,16},{16,24},{24,32},{32,40},{40,48},{48,56},{56,64},{64,7... | collective-permute-start | bytes 786440 | tf_op jit(solution)/shard_map/while/body/eval_jaxpr/ppermute | solution.py:17
  711.5 9.8 %collective-permute-start = (f32[4,128,128]{2,1,0:T(8,128)S(1)}, f32[4,128,128]{2,1,0:T(8,128)S(1)}, u32[]{:S(2)}, u32[]{:S(2)}) collective-permute-start(f32[4,128,128]{2,1,0:T(8,128)S(1)} %convolution_add_fusion.7), channel_id=1, source_target_pairs={{0,8},{8,16},{16,24},{24,32},{32,40},{40,48},{48,56},{56,64},{64,7... | collective-permute-start | bytes 786440 | tf_op jit(solution)/shard_map/while/body/eval_jaxpr/ppermute | solution.py:17
  721.7 9.8 %collective-permute-start = (f32[4,128,128]{2,1,0:T(8,128)S(1)}, f32[4,128,128]{2,1,0:T(8,128)S(1)}, u32[]{:S(2)}, u32[]{:S(2)}) collective-permute-start(f32[4,128,128]{2,1,0:T(8,128)S(1)} %convolution_add_fusion.7), channel_id=1, source_target_pairs={{0,8},{8,16},{16,24},{24,32},{32,40},{40,48},{48,56},{56,64},{64,7... | collective-permute-start | bytes 786440 | tf_op jit(solution)/shard_map/while/body/eval_jaxpr/ppermute | solution.py:17
  731.9 9.8 %collective-permute-start = (f32[4,128,128]{2,1,0:T(8,128)S(1)}, f32[4,128,128]{2,1,0:T(8,128)S(1)}, u32[]{:S(2)}, u32[]{:S(2)}) collective-permute-start(f32[4,128,128]{2,1,0:T(8,128)S(1)} %convolution_add_fusion.7), channel_id=1, source_target_pairs={{0,8},{8,16},{16,24},{24,32},{32,40},{40,48},{48,56},{56,64},{64,7... | collective-permute-start | bytes 786440 | tf_op jit(solution)/shard_map/while/body/eval_jaxpr/ppermute | solution.py:17
  742.1 9.8 %collective-permute-start = (f32[4,128,128]{2,1,0:T(8,128)S(1)}, f32[4,128,128]{2,1,0:T(8,128)S(1)}, u32[]{:S(2)}, u32[]{:S(2)}) collective-permute-start(f32[4,128,128]{2,1,0:T(8,128)S(1)} %convolution_add_fusion.7), channel_id=1, source_target_pairs={{0,8},{8,16},{16,24},{24,32},{32,40},{40,48},{48,56},{56,64},{64,7... | collective-permute-start | bytes 786440 | tf_op jit(solution)/shard_map/while/body/eval_jaxpr/ppermute | solution.py:17
  752.3 9.8 %collective-permute-start = (f32[4,128,128]{2,1,0:T(8,128)S(1)}, f32[4,128,128]{2,1,0:T(8,128)S(1)}, u32[]{:S(2)}, u32[]{:S(2)}) collective-permute-start(f32[4,128,128]{2,1,0:T(8,128)S(1)} %convolution_add_fusion.7), channel_id=1, source_target_pairs={{0,8},{8,16},{16,24},{24,32},{32,40},{40,48},{48,56},{56,64},{64,7... | collective-permute-start | bytes 786440 | tf_op jit(solution)/shard_map/while/body/eval_jaxpr/ppermute | solution.py:17
  762.5 9.8 %collective-permute-start = (f32[4,128,128]{2,1,0:T(8,128)S(1)}, f32[4,128,128]{2,1,0:T(8,128)S(1)}, u32[]{:S(2)}, u32[]{:S(2)}) collective-permute-start(f32[4,128,128]{2,1,0:T(8,128)S(1)} %convolution_add_fusion.7), channel_id=1, source_target_pairs={{0,8},{8,16},{16,24},{24,32},{32,40},{40,48},{48,56},{56,64},{64,7... | collective-permute-start | bytes 786440 | tf_op jit(solution)/shard_map/while/body/eval_jaxpr/ppermute | solution.py:17
  772.7 9.8 %collective-permute-start = (f32[4,128,128]{2,1,0:T(8,128)S(1)}, f32[4,128,128]{2,1,0:T(8,128)S(1)}, u32[]{:S(2)}, u32[]{:S(2)}) collective-permute-start(f32[4,128,128]{2,1,0:T(8,128)S(1)} %convolution_add_fusion.7), channel_id=1, source_target_pairs={{0,8},{8,16},{16,24},{24,32},{32,40},{40,48},{48,56},{56,64},{64,7... | collective-permute-start | bytes 786440 | tf_op jit(solution)/shard_map/while/body/eval_jaxpr/ppermute | solution.py:17
  782.9 9.8 %collective-permute-start = (f32[4,128,128]{2,1,0:T(8,128)S(1)}, f32[4,128,128]{2,1,0:T(8,128)S(1)}, u32[]{:S(2)}, u32[]{:S(2)}) collective-permute-start(f32[4,128,128]{2,1,0:T(8,128)S(1)} %convolution_add_fusion.7), channel_id=1, source_target_pairs={{0,8},{8,16},{16,24},{24,32},{32,40},{40,48},{48,56},{56,64},{64,7... | collective-permute-start | bytes 786440 | tf_op jit(solution)/shard_map/while/body/eval_jaxpr/ppermute | solution.py:17
  793.1 9.8 %collective-permute-start = (f32[4,128,128]{2,1,0:T(8,128)S(1)}, f32[4,128,128]{2,1,0:T(8,128)S(1)}, u32[]{:S(2)}, u32[]{:S(2)}) collective-permute-start(f32[4,128,128]{2,1,0:T(8,128)S(1)} %convolution_add_fusion.7), channel_id=1, source_target_pairs={{0,8},{8,16},{16,24},{24,32},{32,40},{40,48},{48,56},{56,64},{64,7... | collective-permute-start | bytes 786440 | tf_op jit(solution)/shard_map/while/body/eval_jaxpr/ppermute | solution.py:17
  803.3 9.8 %collective-permute-start = (f32[4,128,128]{2,1,0:T(8,128)S(1)}, f32[4,128,128]{2,1,0:T(8,128)S(1)}, u32[]{:S(2)}, u32[]{:S(2)}) collective-permute-start(f32[4,128,128]{2,1,0:T(8,128)S(1)} %convolution_add_fusion.7), channel_id=1, source_target_pairs={{0,8},{8,16},{16,24},{24,32},{32,40},{40,48},{48,56},{56,64},{64,7... | collective-permute-start | bytes 786440 | tf_op jit(solution)/shard_map/while/body/eval_jaxpr/ppermute | solution.py:17
  813.5 9.8 %collective-permute-start = (f32[4,128,128]{2,1,0:T(8,128)S(1)}, f32[4,128,128]{2,1,0:T(8,128)S(1)}, u32[]{:S(2)}, u32[]{:S(2)}) collective-permute-start(f32[4,128,128]{2,1,0:T(8,128)S(1)} %convolution_add_fusion.7), channel_id=1, source_target_pairs={{0,8},{8,16},{16,24},{24,32},{32,40},{40,48},{48,56},{56,64},{64,7... | collective-permute-start | bytes 786440 | tf_op jit(solution)/shard_map/while/body/eval_jaxpr/ppermute | solution.py:17
  823.7 9.8 %collective-permute-start = (f32[4,128,128]{2,1,0:T(8,128)S(1)}, f32[4,128,128]{2,1,0:T(8,128)S(1)}, u32[]{:S(2)}, u32[]{:S(2)}) collective-permute-start(f32[4,128,128]{2,1,0:T(8,128)S(1)} %convolution_add_fusion.7), channel_id=1, source_target_pairs={{0,8},{8,16},{16,24},{24,32},{32,40},{40,48},{48,56},{56,64},{64,7... | collective-permute-start | bytes 786440 | tf_op jit(solution)/shard_map/while/body/eval_jaxpr/ppermute | solution.py:17
  833.9 9.8 %collective-permute-start = (f32[4,128,128]{2,1,0:T(8,128)S(1)}, f32[4,128,128]{2,1,0:T(8,128)S(1)}, u32[]{:S(2)}, u32[]{:S(2)}) collective-permute-start(f32[4,128,128]{2,1,0:T(8,128)S(1)} %convolution_add_fusion.7), channel_id=1, source_target_pairs={{0,8},{8,16},{16,24},{24,32},{32,40},{40,48},{48,56},{56,64},{64,7... | collective-permute-start | bytes 786440 | tf_op jit(solution)/shard_map/while/body/eval_jaxpr/ppermute | solution.py:17
  844.1 9.8 %collective-permute-start = (f32[4,128,128]{2,1,0:T(8,128)S(1)}, f32[4,128,128]{2,1,0:T(8,128)S(1)}, u32[]{:S(2)}, u32[]{:S(2)}) collective-permute-start(f32[4,128,128]{2,1,0:T(8,128)S(1)} %convolution_add_fusion.7), channel_id=1, source_target_pairs={{0,8},{8,16},{16,24},{24,32},{32,40},{40,48},{48,56},{56,64},{64,7... | collective-permute-start | bytes 786440 | tf_op jit(solution)/shard_map/while/body/eval_jaxpr/ppermute | solution.py:17
  854.3 9.8 %collective-permute-start = (f32[4,128,128]{2,1,0:T(8,128)S(1)}, f32[4,128,128]{2,1,0:T(8,128)S(1)}, u32[]{:S(2)}, u32[]{:S(2)}) collective-permute-start(f32[4,128,128]{2,1,0:T(8,128)S(1)} %convolution_add_fusion.7), channel_id=1, source_target_pairs={{0,8},{8,16},{16,24},{24,32},{32,40},{40,48},{48,56},{56,64},{64,7... | collective-permute-start | bytes 786440 | tf_op jit(solution)/shard_map/while/body/eval_jaxpr/ppermute | solution.py:17
where the time goes:
time: 951 us; the launch traced here: 940 us
  other arithmetic  336 us (35%)
  waiting for transfers between devices  308 us (32%)
  matrix products  150 us (16%)
  starting transfers between devices  90.8 us (10%)
  blocking collectives  27.5 us (3%)
  local copies, waits for them, and re-layouts  25.2 us (3%)
    another operation x2, other arithmetic, block_maps(): jax.scipy.linalg.solve_triangular(system, jnp.concatenate([value_blk, key...  316 us
    ppermute x31, waiting for transfers between devices, shifted_2(): return lax.ppermute(x, axis, pairs)  229 us
    ppermute x31, starting transfers between devices, shifted_2(): return lax.ppermute(x, axis, pairs)  67.7 us
    all_to_all x1, waiting for transfers between devices, local(): lax.all_to_all(log_decay, 'head', split_axis=1, concat_axis=0, tiled=True)  28 us
    all_to_all x1, blocking collectives, local(): lax.all_to_all(grouped, 'head', split_axis=0, concat_axis=1, tiled=True)  27.5 us
    all_to_all x1, waiting for transfers between devices, local(): lax.all_to_all(key_rows, 'head', split_axis=1, concat_axis=0, tiled=True)  26.4 us
    dot_general x16, matrix products, compose(): jnp.einsum('...de,...ef->...df', later[0], earlier[1], precision=highest)  22.8 us
    dot_general x16, matrix products, run_state(): jnp.einsum('hde,hef->hdf', move_blk, memory, precision=highest) + carry_blk  22.8 us
  transfers between devices with their start and end apart: 36, of which 35 were waited for; matrix products, arithmetic and copies ran while one was open for 38% of the time, Pallas kernels for 0%

commit v1 on v0

v1 whole, which is shorter than its diff:
```python
import functools

import jax
import jax.numpy as jnp
from jax import lax
from jax.experimental import pallas as pl
from jax.experimental.pallas import tpu as pltpu
from jax.sharding import PartitionSpec as P

DK = 128
L = 128
F32 = jnp.float32
BF = jnp.bfloat16
MESH = pl.DeviceIdType.MESH


def split(x):
    hi = x.astype(BF)
    return hi, (x - hi.astype(F32)).astype(BF)


def mm(a, b, dims=((1,), (0,))):
    return lax.dot_general(a, b, (dims, ((), ())), preferred_element_type=F32)


def dot3(a, b, turned=False):
    dims = ((1,), (1,)) if turned else ((1,), (0,))
    wide = jnp.concatenate([a[0], a[1]], 1)
    twice = jnp.concatenate([b[0], b[0]], 1 if turned else 0)
    return mm(wide, twice, dims) + mm(a[0], b[1], dims)


def dot2(a, b):
    return mm(jnp.concatenate([a[0], a[1]], 1), jnp.concatenate([b, b], 0))


def unit_rows(x):
    return x * lax.rsqrt(jnp.sum(x * x, axis=-1, keepdims=True) + 1e-6)


def block_maps(units):
    row = lax.broadcasted_iota(jnp.int32, (L, L), 0)
    col = lax.broadcasted_iota(jnp.int32, (L, L), 1)
    eye = row == col
    tri = (row >= col).astype(BF)
    pre = []
    for q, k, v, g, rate in units:
        cum = mm(tri, g)
        qn = unit_rows(q.astype(F32))
        kn = unit_rows(k.astype(F32))
        mid = cum[L // 2 : L // 2 + 1, :]
        closing = cum[L - 1 : L, :]
        up = jnp.exp(cum - mid)
        past = jnp.exp(cum)
        kr = kn * rate
        pre.append(
            (
                split(jnp.concatenate([kn * up, qn * up], 0)),
                split(kr * jnp.exp(mid - cum)),
                split(kn * past),
                jnp.concatenate([qn * past, jnp.where(eye, jnp.exp(closing), 0.0)], 0),
                (kr * jnp.exp(closing - cum)).T,
                v,
            )
        )
    pairs = [dot3(p[0], p[1], True) for p in pre]
    among = [jnp.where(row > col, m[:L], 0.0) for m in pairs]
    attend = [jnp.where(row >= col, m[L:], 0.0) for m in pairs]
    inverse = None
    size = 1
    while size < L:
        lower = jnp.logical_and(
            row // (2 * size) == col // (2 * size),
            jnp.logical_and((row // size) % 2 == 1, (col // size) % 2 == 0),
        )
        if inverse is None:
            inverse = [jnp.where(eye, 1.0, 0.0) - jnp.where(lower, a, 0.0) for a in among]
        else:
            halves = [split(x) for x in inverse]
            right = [
                split(dot3(split(jnp.where(lower, a, 0.0)), x)) for a, x in zip(among, halves)
            ]
            inverse = [x - dot3(h, r) for x, h, r in zip(inverse, halves, right)]
        size *= 2
    both = [
        split(dot3(split(jnp.concatenate([a, p[4]], 0)), split(x)))
        for a, p, x in zip(attend, pre, inverse)
    ]
    return [(p[3] - dot3(z, p[2]), dot2(z, p[5])) for z, p in zip(both, pre)]


def compose(later, earlier):
    product = dot3(split(later[:, :DK]), split(earlier))
    return jnp.concatenate([product[:, :DK], product[:, DK:] + later[:, DK:]], 1)


def advance(span, state):
    return dot3(split(span[:, :DK]), split(state)) + span[:, DK:]


def head_maps(q_ref, k_ref, v_ref, g_ref, rate_ref, ab_ref, tc_ref, group):
    blocks = q_ref.shape[0] // L
    prefix = None
    for first in range(0, blocks, group):
        rows = [pl.ds(b * L, L) for b in range(first, first + group)]
        maps = block_maps(
            [(q_ref[r, :], k_ref[r, :], v_ref[r, :], g_ref[r, :], rate_ref[r, :]) for r in rows]
        )
        for r, (moves, adds) in zip(rows, maps):
            if prefix is None:
                both = jnp.concatenate([moves, adds], 1)
            else:
                both = dot3(split(moves), split(prefix))
                both = jnp.concatenate([both[:, :DK], both[:, DK:] + adds], 1)
            ab_ref[r, :] = both[:L]
            prefix = both[L:]
    tc_ref[...] = prefix


def maps_kernel(q_ref, k_ref, v_ref, g_ref, rate_ref, ab_ref, tc_ref):
    head_maps(q_ref, k_ref, v_ref, g_ref, rate_ref.at[0], ab_ref.at[0], tc_ref.at[0], 8)


def scan_kernel(
    tc_ref, ab_ref, out_ref, sib, chip, xb, yb, enter, send_sem, recv_sem
):
    me = lax.axis_index("seq")
    z = lax.axis_index("head")
    core, x, y = me % 2, (me // 2) % 4, me // 8
    peer = me + 1 - 2 * core
    x_peers = [y * 8 + ((x + d) % 4) * 2 + core for d in (1, 2, 3)]
    y_peers = [((y + d) % 4) * 8 + x * 2 + core for d in (1, 2, 3)]
    barrier = pltpu.get_barrier_semaphore()
    for to in [peer] + x_peers + y_peers:
        pl.semaphore_signal(barrier, inc=1, device_id=(to, z), device_id_type=MESH)
    pl.semaphore_wait(barrier, 7)

    def copy(src, dst, j, n, to):
        return pltpu.make_async_remote_copy(
            src_ref=src,
            dst_ref=dst,
            send_sem=send_sem.at[j, n],
            recv_sem=recv_sem.at[j, n],
            device_id=(to, z),
            device_id_type=MESH,
        )

    live = []
    for j in range(2):
        c = copy(tc_ref.at[2 * j + 1 - core], sib.at[j], j, 0, peer)
        c.start()
        live.append(c)
    firsts = []
    for j in range(2):
        live[j].wait_recv()
        own, other = tc_ref[2 * j + core], sib[j]
        first = jnp.where(core == 0, own, other)
        chip[j] = compose(jnp.where(core == 0, other, own), first)
        firsts.append(first)
        for d in range(3):
            c = copy(chip.at[j], xb.at[j, d], j, 1 + d, x_peers[d])
            c.start()
            live.append(c)
    befores = []
    for j in range(2):
        for d in range(3):
            live[2 + 3 * j + d].wait_recv()
        spans = []
        for i in range(4):
            far = (x - i + 4) % 4
            spans.append(
                jnp.where(
                    far == 0,
                    chip[j],
                    jnp.where(far == 1, xb[j, 0], jnp.where(far == 2, xb[j, 1], xb[j, 2])),
                )
            )
        two = compose(spans[1], spans[0])
        three = compose(spans[2], two)
        total = compose(compose(spans[3], spans[2]), two)
        befores.append((spans[0], two, three))
        yb[j, 3] = total
        for d in range(3):
            c = copy(yb.at[j, 3], yb.at[j, d], j, 4 + d, y_peers[d])
            c.start()
            live.append(c)
    for j in range(2):
        for d in range(3):
            live[8 + 3 * j + d].wait_recv()
        spans = []
        for i in range(3):
            far = (y - i + 4) % 4
            spans.append(
                jnp.where(
                    far == 0,
                    yb[j, 3],
                    jnp.where(far == 1, yb[j, 0], jnp.where(far == 2, yb[j, 1], yb[j, 2])),
                )
            )
        one = spans[0][:, DK:]
        two = advance(spans[1], one)
        three = advance(spans[2], two)
        state = jnp.where(y == 0, 0.0, jnp.where(y == 1, one, jnp.where(y == 2, two, three)))
        before = jnp.where(
            x == 1, befores[j][0], jnp.where(x == 2, befores[j][1], befores[j][2])
        )
        state = jnp.where(x == 0, state, advance(before, state))
        after = advance(firsts[j], state)
        enter[j, 0] = jnp.where(core == 0, state, after)
        enter[j, 1] = jnp.where(core == 0, after, state)
        c = copy(enter.at[j, 1], enter.at[j, 2], j, 7, peer)
        c.start()
        live.append(c)
    for j in range(2):
        live[14 + j].wait_recv()
        for half in range(2):
            h = 2 * j + half
            state = jnp.where(core == half, enter[j, 0], enter[j, 2])
            ab = ab_ref[h]
            out = dot3(split(ab[:, :DK]), split(state)) + ab[:, DK:]
            out_ref[:, h * DK : (h + 1) * DK] = out.astype(BF)
    for c in live:
        c.wait_send()


def local(query_rows, key_rows, value_rows, log_decay, write_rate):
    def moved(a):
        return lax.all_to_all(a, "head", split_axis=1, concat_axis=0, tiled=True)

    rate = moved(write_rate).astype(F32).T[:, :, None]
    g, k, v, q = moved(log_decay), moved(key_rows), moved(value_rows), moved(query_rows)
    rows, heads = g.shape[0], g.shape[1] // DK
    cols = pl.BlockSpec((rows, DK), lambda h: (0, h))
    ab, tc = pl.pallas_call(
        maps_kernel,
        grid=(heads,),
        in_specs=[cols] * 4 + [pl.BlockSpec((1, rows, 1), lambda h: (h, 0, 0))],
        out_specs=[
            pl.BlockSpec((1, rows, 2 * DK), lambda h: (h, 0, 0)),
            pl.BlockSpec((1, DK, 2 * DK), lambda h: (h, 0, 0)),
        ],
        out_shape=[
            jax.ShapeDtypeStruct((heads, rows, 2 * DK), F32),
            jax.ShapeDtypeStruct((heads, DK, 2 * DK), F32),
        ],
        compiler_params=pltpu.CompilerParams(vmem_limit_bytes=48 * 2**20),
    )(q, k, v, g, rate)
    whole = pl.BlockSpec(memory_space=pltpu.VMEM)
    out = pl.pallas_call(
        scan_kernel,
        in_specs=[whole, whole],
        out_specs=whole,
        out_shape=jax.ShapeDtypeStruct((rows, heads * DK), BF),
        scratch_shapes=[
            pltpu.VMEM((2, DK, 2 * DK), F32),
            pltpu.VMEM((2, DK, 2 * DK), F32),
            pltpu.VMEM((2, 3, DK, 2 * DK), F32),
            pltpu.VMEM((2, 4, DK, 2 * DK), F32),
            pltpu.VMEM((2, 3, DK, DK), F32),
            pltpu.SemaphoreType.DMA((2, 8)),
            pltpu.SemaphoreType.DMA((2, 8)),
        ],
        compiler_params=pltpu.CompilerParams(
            vmem_limit_bytes=48 * 2**20, collective_id=0, has_side_effects=True
        ),
    )(tc, ab)
    return lax.all_to_all(out, "head", split_axis=0, concat_axis=1, tiled=True)


def solution(mesh):
    spec = P(("seq", "head"), None)
    return jax.shard_map(
        local, mesh=mesh, in_specs=(spec,) * 5, out_specs=spec, check_vma=False
    )
```

time: 951 us -> 242 us (0.25)
  other arithmetic: 336 us -> 0.01 us
  waiting for transfers between devices: 308 us -> 114 us
  matrix products: 150 us -> 0 us
  starting transfers between devices: 90.8 us -> 23.2 us
  Pallas kernels: 0 us -> 58.4 us
  local copies, waits for them, and re-layouts: 25.2 us -> 12.1 us
    another operation x3 -> x0, other arithmetic: 317 us -> none  [the longest x2 316 us: block_maps(): jax.scipy.linalg.solve_triangular(system, jnp.concatenate([value_blk, key...]
    ppermute x31 -> x0, waiting for transfers between devices: 229 us -> none  [shifted_2(): return lax.ppermute(x, axis, pairs)]
    dot_general x101 -> x0, matrix products: 146 us -> none  [the longest x16 22.8 us: compose(): jnp.einsum('...de,...ef->...df', later[0], earlier[1], precision=highest)]
    ppermute x31 -> x0, starting transfers between devices: 67.7 us -> none  [shifted_2(): return lax.ppermute(x, axis, pairs)]
    pallas_call x0 -> x2, Pallas kernels: none -> 58.4 us  [the longest x1 30 us: local(): pl.pallas_call(scan_kernel, in_specs=[whole, whole], out_specs=whole, out...]
    all_to_all x5, waiting for transfers between devices: 78.2 us -> 114 us  [moved(): return lax.all_to_all(a, 'head', split_axis=1, concat_axis=0, tiled=True)]
    convert_element_type x10 -> x0, local copies, waits for them, and re-layouts: 15.4 us -> none  [the longest x5 14 us: to_blocks(): return matrix.reshape(rows // BLOCK, BLOCK, heads_here, -1).transpose(0,...]
    convert_element_type x7 -> x0, other arithmetic: 10.2 us -> none  [the longest x4 8.94 us: to_blocks(): return matrix.reshape(rows // BLOCK, BLOCK, heads_here, -1).transpose(0,...]
  transfers between devices with their start and end apart: 36 -> 5, of which waited for: 35 -> 5; matrix products, arithmetic and copies ran while one was open for 38% -> 4% of each run, Pallas kernels for 0% -> 0%
where the time goes in v1:
time: 242 us; the launch traced here: 240 us
  waiting for transfers between devices  114 us (47%)
  Pallas kernels  58.4 us (24%)
  blocking collectives  31.7 us (13%)
  starting transfers between devices  23.2 us (10%)
  local copies, waits for them, and re-layouts  12.1 us (5%)
    all_to_all x5, waiting for transfers between devices, moved(): return lax.all_to_all(a, 'head', split_axis=1, concat_axis=0, tiled=True)  114 us
    all_to_all x1, blocking collectives, local(): return lax.all_to_all(out, 'head', split_axis=0, concat_axis=1, tiled=True)  31.7 us
    pallas_call x1, Pallas kernels, local(): pl.pallas_call(scan_kernel, in_specs=[whole, whole], out_specs=whole, out...  30 us
    pallas_call x1, Pallas kernels, local(): pl.pallas_call(maps_kernel, grid=(heads,), in_specs=[cols] * 4 + [pl.Bloc...  28.4 us
    all_to_all x5, starting transfers between devices, moved(): return lax.all_to_all(a, 'head', split_axis=1, concat_axis=0, tiled=True)  23.2 us
    all_to_all x4, local copies, waits for them, and re-layouts, moved(): return lax.all_to_all(a, 'head', split_axis=1, concat_axis=0, tiled=True)  6.82 us
  transfers between devices with their start and end apart: 5, of which 5 were waited for; matrix products, arithmetic and copies ran while one was open for 4% of the time, Pallas kernels for 0%

profile of v1, /device:TPU:17, one launch (start us, length us, event | category | flops | bytes accessed | tf_op | source)
XLA Modules:
  0.0 239.8 jit_solution(6080822048987481029)
XLA Ops:
  0.0 0.0 copy-start.1
  0.0 8.3 %all-to-all-start.4 = ((bf16[128,8,4]{0,2,1:T(4,128)(2,1)}), bf16[128,8,4]{0,2,1:T(4,128)(2,1)S(1)}, u32[]{:S(2)}, u32[]{:S(2)}) async-start(bf16[128,8,4]{0,2,1:T(4,128)(2,1)} %bitcast.52), calls=%async_computation.4 | async-start | bytes 16384 | tf_op jit(solution)/shard_map/all_to_all | solution.py:228
  8.3 0.0 copy-start.2
  8.3 2.4 copy.30
  10.7 4.2 %all-to-all-done.4 = bf16[128,8,4]{0,2,1:T(4,128)(2,1)S(1)} async-done(((bf16[128,8,4]{0,2,1:T(4,128)(2,1)}), bf16[128,8,4]{0,2,1:T(4,128)(2,1)S(1)}, u32[]{:S(2)}, u32[]{:S(2)}) %all-to-all-start.4) | async-done | bytes 8224 | tf_op jit(solution)/shard_map/all_to_all | solution.py:228
  14.9 3.6 %all-to-all-start = ((bf16[128,8,512]{2,0,1:T(8,128)(2,1)}), bf16[128,8,512]{2,0,1:T(8,128)(2,1)S(1)}, u32[]{:S(2)}, u32[]{:S(2)}) async-start(bf16[128,8,512]{2,0,1:T(8,128)(2,1)} %bitcast.40), calls=%async_computation | async-start | bytes 2097152 | tf_op jit(solution)/shard_map/all_to_all | solution.py:228
  18.5 0.0 copy-done.1
  18.5 1.1 copy.29
  19.5 28.0 %all-to-all-done = bf16[128,8,512]{2,0,1:T(8,128)(2,1)S(1)} async-done(((bf16[128,8,512]{2,0,1:T(8,128)(2,1)}), bf16[128,8,512]{2,0,1:T(8,128)(2,1)S(1)}, u32[]{:S(2)}, u32[]{:S(2)}) %all-to-all-start) | async-done | bytes 1048608 | tf_op jit(solution)/shard_map/all_to_all | solution.py:228
  47.6 3.6 %all-to-all-start.1 = ((bf16[128,8,512]{2,0,1:T(8,128)(2,1)}), bf16[128,8,512]{2,0,1:T(8,128)(2,1)S(1)}, u32[]{:S(2)}, u32[]{:S(2)}) async-start(bf16[128,8,512]{2,0,1:T(8,128)(2,1)} %bitcast.39), calls=%async_computation.1 | async-start | bytes 2097152 | tf_op jit(solution)/shard_map/all_to_all | solution.py:228
  51.1 0.0 copy-done.2
  51.1 1.1 copy.28
  52.2 28.1 %all-to-all-done.1 = bf16[128,8,512]{2,0,1:T(8,128)(2,1)S(1)} async-done(((bf16[128,8,512]{2,0,1:T(8,128)(2,1)}), bf16[128,8,512]{2,0,1:T(8,128)(2,1)S(1)}, u32[]{:S(2)}, u32[]{:S(2)}) %all-to-all-start.1) | async-done | bytes 1048608 | tf_op jit(solution)/shard_map/all_to_all | solution.py:228
  80.3 3.6 %all-to-all-start.2 = ((bf16[128,8,512]{2,0,1:T(8,128)(2,1)}), bf16[128,8,512]{2,0,1:T(8,128)(2,1)S(1)}, u32[]{:S(2)}, u32[]{:S(2)}) async-start(bf16[128,8,512]{2,0,1:T(8,128)(2,1)} %bitcast.46), calls=%async_computation.2 | async-start | bytes 2097152 | tf_op jit(solution)/shard_map/all_to_all | solution.py:228
  83.9 2.3 copy.27
  86.2 26.9 %all-to-all-done.2 = bf16[128,8,512]{2,0,1:T(8,128)(2,1)S(1)} async-done(((bf16[128,8,512]{2,0,1:T(8,128)(2,1)}), bf16[128,8,512]{2,0,1:T(8,128)(2,1)S(1)}, u32[]{:S(2)}, u32[]{:S(2)}) %all-to-all-start.2) | async-done | bytes 1048608 | tf_op jit(solution)/shard_map/all_to_all | solution.py:228
  113.0 4.2 %all-to-all-start.3 = ((bf16[128,8,512]{2,0,1:T(8,128)(2,1)}), bf16[128,8,512]{2,0,1:T(8,128)(2,1)}, u32[]{:S(2)}, u32[]{:S(2)}) async-start(bf16[128,8,512]{2,0,1:T(8,128)(2,1)} %bitcast.45), calls=%async_computation.3 | async-start | bytes 2097152 | tf_op jit(solution)/shard_map/all_to_all | solution.py:228
  117.3 2.0 copy.16.rate_ref
  119.2 27.2 %all-to-all-done.3 = bf16[128,8,512]{2,0,1:T(8,128)(2,1)} async-done(((bf16[128,8,512]{2,0,1:T(8,128)(2,1)}), bf16[128,8,512]{2,0,1:T(8,128)(2,1)}, u32[]{:S(2)}, u32[]{:S(2)}) %all-to-all-start.3) | async-done | bytes 1048608 | tf_op jit(solution)/shard_map/all_to_all | solution.py:228
  146.5 28.4 %shard_map.55 = (f32[4,1024,256]{2,1,0:T(8,128)}, f32[4,128,256]{2,1,0:T(8,128)S(1)}) custom-call(bf16[1024,512]{1,0:T(8,128)(2,1)S(1)} %bitcast.41, bf16[1024,512]{1,0:T(8,128)(2,1)S(1)} %bitcast.42, bf16[1024,512]{1,0:T(8,128)(2,1)S(1)} %bitcast.43, bf16[1024,512]{1,0:T(8,128)(2,1)} %bitcast.7.g_ref, f32[4,1024,1]{2,1,0:T(8,128)} %copy.16.rate_ref), custom_call_target="tpu_custom_call" | custom-call | tf_op jit(solution)/shard_map/pallas_call | solution.py:234
  174.9 0.0 copy-start
  174.9 2.2 copy-done
  177.1 30.0 %shard_map.56 = bf16[1024,512]{1,0:T(8,128)(2,1)S(1)} custom-call(f32[4,128,256]{2,1,0:T(8,128)S(1)} %get-tuple-element.7.tc_ref, f32[4,1024,256]{2,1,0:T(8,128)S(1)} %copy-done), custom_call_target="tpu_custom_call" | custom-call | tf_op jit(solution)/shard_map/pallas_call | solution.py:249
  207.0 31.7 %all_to_all.108 = bf16[8,128,512]{2,1,0:T(8,128)(2,1)S(1)} all-to-all(bf16[8,128,512]{2,1,0:T(8,128)(2,1)S(1)} %bitcast.44), channel_id=1, replica_groups=mesh['seq'=32,'head'=8] {'head'}, dimensions={0} | all-to-all | bytes 2097152 | tf_op jit(solution)/shard_map/all_to_all | solution.py:267
  238.7 1.1 copy.22
  (1 shorter events, 0.0 us)
Async XLA Ops:
  0.0 18.5 %copy-start.1 = (bf16[128,4096]{1,0:T(8,128)(2,1)S(1)}, bf16[128,4096]{1,0:T(8,128)(2,1)}, u32[]{:S(2)}) copy-start(bf16[128,4096]{1,0:T(8,128)(2,1)} %param.6) | copy-start | bytes 3145732
  0.0 14.9 %all-to-all-start.4 = ((bf16[128,8,4]{0,2,1:T(4,128)(2,1)}), bf16[128,8,4]{0,2,1:T(4,128)(2,1)S(1)}, u32[]{:S(2)}, u32[]{:S(2)}) async-start(bf16[128,8,4]{0,2,1:T(4,128)(2,1)} %bitcast.52), calls=%async_computation.4 | async-start | bytes 16384 | tf_op jit(solution)/shard_map/all_to_all | solution.py:228
  8.3 42.8 %copy-start.2 = (bf16[128,4096]{1,0:T(8,128)(2,1)S(1)}, bf16[128,4096]{1,0:T(8,128)(2,1)}, u32[]{:S(2)}) copy-start(bf16[128,4096]{1,0:T(8,128)(2,1)} %param.7) | copy-start | bytes 3145732
  14.9 32.7 %all-to-all-start = ((bf16[128,8,512]{2,0,1:T(8,128)(2,1)}), bf16[128,8,512]{2,0,1:T(8,128)(2,1)S(1)}, u32[]{:S(2)}, u32[]{:S(2)}) async-start(bf16[128,8,512]{2,0,1:T(8,128)(2,1)} %bitcast.40), calls=%async_computation | async-start | bytes 2097152 | tf_op jit(solution)/shard_map/all_to_all | solution.py:228
  47.6 32.7 %all-to-all-start.1 = ((bf16[128,8,512]{2,0,1:T(8,128)(2,1)}), bf16[128,8,512]{2,0,1:T(8,128)(2,1)S(1)}, u32[]{:S(2)}, u32[]{:S(2)}) async-start(bf16[128,8,512]{2,0,1:T(8,128)(2,1)} %bitcast.39), calls=%async_computation.1 | async-start | bytes 2097152 | tf_op jit(solution)/shard_map/all_to_all | solution.py:228
  80.3 32.7 %all-to-all-start.2 = ((bf16[128,8,512]{2,0,1:T(8,128)(2,1)}), bf16[128,8,512]{2,0,1:T(8,128)(2,1)S(1)}, u32[]{:S(2)}, u32[]{:S(2)}) async-start(bf16[128,8,512]{2,0,1:T(8,128)(2,1)} %bitcast.46), calls=%async_computation.2 | async-start | bytes 2097152 | tf_op jit(solution)/shard_map/all_to_all | solution.py:228
  113.0 33.5 %all-to-all-start.3 = ((bf16[128,8,512]{2,0,1:T(8,128)(2,1)}), bf16[128,8,512]{2,0,1:T(8,128)(2,1)}, u32[]{:S(2)}, u32[]{:S(2)}) async-start(bf16[128,8,512]{2,0,1:T(8,128)(2,1)} %bitcast.45), calls=%async_computation.3 | async-start | bytes 2097152 | tf_op jit(solution)/shard_map/all_to_all | solution.py:228
  174.9 2.2 copy-start

commit v2 on v1

v2 whole, which is shorter than its diff:
```python
import functools

import jax
import jax.numpy as jnp
from jax import lax
from jax.experimental import pallas as pl
from jax.experimental.pallas import tpu as pltpu
from jax.sharding import PartitionSpec as P

DK = 128
L = 128
RING = 8
HEADS = 4
GROUP = 4
F32 = jnp.float32
BF = jnp.bfloat16
MESH = pl.DeviceIdType.MESH


def split(x):
    hi = x.astype(BF)
    return hi, (x - hi.astype(F32)).astype(BF)


def mm(a, b, dims=((1,), (0,))):
    return lax.dot_general(a, b, (dims, ((), ())), preferred_element_type=F32)


def dot3(a, b, turned=False):
    dims = ((1,), (1,)) if turned else ((1,), (0,))
    wide = jnp.concatenate([a[0], a[1]], 1)
    twice = jnp.concatenate([b[0], b[0]], 1 if turned else 0)
    return mm(wide, twice, dims) + mm(a[0], b[1], dims)


def dot2(a, b):
    return mm(jnp.concatenate([a[0], a[1]], 1), jnp.concatenate([b, b], 0))


def unit_rows(x):
    return x * lax.rsqrt(jnp.sum(x * x, axis=-1, keepdims=True) + 1e-6)


def masks():
    row = lax.broadcasted_iota(jnp.int32, (L, L), 0)
    col = lax.broadcasted_iota(jnp.int32, (L, L), 1)
    return row, col


def unit_inverse(among):
    row, col = masks()
    eye = jnp.where(row == col, 1.0, 0.0)
    inverse = None
    size = 1
    while size < L:
        lower = jnp.logical_and(
            row // (2 * size) == col // (2 * size),
            jnp.logical_and((row // size) % 2 == 1, (col // size) % 2 == 0),
        )
        if inverse is None:
            inverse = [eye - jnp.where(lower, a, 0.0) for a in among]
        else:
            halves = [split(x) for x in inverse]
            right = [
                split(dot3(split(jnp.where(lower, a, 0.0)), x)) for a, x in zip(among, halves)
            ]
            inverse = [x - dot3(h, r) for x, h, r in zip(inverse, halves, right)]
        size *= 2
    return inverse


def running(g):
    row, col = masks()
    cum = mm((row >= col).astype(BF), g)
    return cum, cum[L // 2 : L // 2 + 1, :], cum[L - 1 : L, :]


def compose(later, earlier):
    product = dot3(split(later[:, :DK]), split(earlier))
    return jnp.concatenate([product[:, :DK], product[:, DK:] + later[:, DK:]], 1)


def advance(span, state):
    return dot3(split(span[:, :DK]), split(state)) + span[:, DK:]


def kernel(
    q_ref, k_ref, v_ref, g_ref, rate_ref, out_ref,
    kb, gb, vb, qb, rb, ob, inv, past, behind, spans,
    sib, chip, first, xb, before, yb, enter,
    in_send, in_recv, out_send, out_recv, rate_send, rate_recv, scan_send, scan_recv,
):
    me = lax.axis_index("seq")
    z = lax.axis_index("head")
    core, x, y = me % 2, (me // 2) % 4, me // 8
    peer = me + 1 - 2 * core
    x_peers = [y * 8 + ((x + d) % 4) * 2 + core for d in (1, 2, 3)]
    y_peers = [((y + d) % 4) * 8 + x * 2 + core for d in (1, 2, 3)]
    row, col = masks()
    eye = row == col

    barrier = pltpu.get_barrier_semaphore()

    def greet(d, carry):
        pl.semaphore_signal(barrier, inc=1, device_id=(me, (z + d) % RING), device_id_type=MESH)
        return carry

    lax.fori_loop(1, RING, greet, 0)
    for to in [peer] + x_peers + y_peers:
        pl.semaphore_signal(barrier, inc=1, device_id=(to, z), device_id_type=MESH)
    pl.semaphore_wait(barrier, RING + 6)

    def columns(owner, h):
        return pl.ds(pl.multiple_of((owner * HEADS + h) * DK, DK), DK)

    def remote(src, dst, send, recv, to):
        return pltpu.make_async_remote_copy(
            src_ref=src, dst_ref=dst, send_sem=send, recv_sem=recv, device_id=to, device_id_type=MESH
        )

    arrays = ((k_ref, kb), (g_ref, gb), (v_ref, vb), (q_ref, qb))

    def incoming(a, h, d):
        to = (z + d) % RING
        src, dst = arrays[a]
        return remote(
            src.at[:, columns(to, h)], dst.at[h, d], in_send.at[a, h, d], in_recv.at[a, h, d], (me, to)
        )

    def own_block(a, h):
        src, dst = arrays[a]
        return pltpu.make_async_copy(src.at[:, columns(z, h)], dst.at[h, 0], in_recv.at[a, h, 0])

    def rates(d):
        to = (z + d) % RING
        return remote(rate_ref, rb.at[d], rate_send.at[d], rate_recv.at[d], (me, to))

    def outgoing(h, d):
        to = (z + d) % RING
        return remote(
            ob.at[h, d], out_ref.at[:, columns(z, h)], out_send.at[h, d], out_recv.at[h, d], (me, to)
        )

    def own_out(h):
        return pltpu.make_async_copy(ob.at[h, 0], out_ref.at[:, columns(z, h)], out_recv.at[h, 0])

    own_rate = pltpu.make_async_copy(rate_ref, rb.at[0], rate_recv.at[0])

    def over_peers(act):
        def one(d, carry):
            act(d)
            return carry

        lax.fori_loop(1, RING, one, 0)

    def start_in(which, h):
        for a in which:
            own_block(a, h).start()
            over_peers(lambda d: incoming(a, h, d).start())

    def wait_in(which, h):
        for a in which:
            own_block(a, h).wait()
            over_peers(lambda d: incoming(a, h, d).wait_recv())

    own_rate.start()
    over_peers(lambda d: rates(d).start())

    def send_three(h, carry):
        start_in((0, 1, 2), h)
        return carry

    def send_query(h, carry):
        start_in((3,), h)
        return carry

    lax.fori_loop(0, HEADS, send_three, 0)
    lax.fori_loop(0, HEADS, send_query, 0)
    own_rate.wait()
    over_peers(lambda d: rates(d).wait_recv())

    def maps(h):
        spans[h, 0] = jnp.concatenate([jnp.where(eye, 1.0, 0.0), jnp.zeros((L, DK), F32)], 1)
        lane = lax.broadcasted_iota(jnp.int32, (L, rb.shape[2]), 1)
        mine = lane == z * HEADS + h

        def group(n, carry):
            pre = []
            for i in range(GROUP):
                b = n * GROUP + i
                slot = (z - b + RING) % RING
                rate = jnp.sum(
                    jnp.where(mine, rb[slot].astype(F32), 0.0), axis=1, keepdims=True
                )
                cum, mid, closing = running(gb[h, slot])
                kn = unit_rows(kb[h, slot].astype(F32))
                kr = kn * rate
                back = kr * jnp.exp(mid - cum)
                kp = kn * jnp.exp(cum)
                behind[h, b] = back
                past[h, b] = kp
                pre.append(
                    (
                        split(kn * jnp.exp(cum - mid)),
                        split(back),
                        split(kp),
                        split((kr * jnp.exp(closing - cum)).T),
                        jnp.where(eye, jnp.exp(closing), 0.0),
                        vb[h, slot],
                    )
                )
            among = [jnp.where(row > col, dot3(p[0], p[1], True), 0.0) for p in pre]
            inverse = unit_inverse(among)
            steps = []
            for i in range(GROUP):
                inv[h, n * GROUP + i] = inverse[i]
                reach = split(dot3(pre[i][3], split(inverse[i])))
                steps.append((pre[i][4] - dot3(reach, pre[i][2]), dot2(reach, pre[i][5])))
            prefix = spans[h, n * GROUP]
            for i in range(GROUP):
                prefix = compose(jnp.concatenate(steps[i], 1), prefix)
                spans[h, n * GROUP + i + 1] = prefix
            return carry

        lax.fori_loop(0, RING // GROUP, group, 0)

    def read_out(h, state):
        halves = split(state)

        def group(n, carry):
            entry, update = [], []
            for i in range(GROUP):
                b = n * GROUP + i
                slot = (z - b + RING) % RING
                span = spans[h, b]
                s = dot3(split(span[:, :DK]), halves) + span[:, DK:]
                entry.append(s)
            for i in range(GROUP):
                b = n * GROUP + i
                slot = (z - b + RING) % RING
                rest = vb[h, slot].astype(F32) - dot3(split(past[h, b]), split(entry[i]))
                update.append(dot3(split(inv[h, b]), split(rest)))
            for i in range(GROUP):
                b = n * GROUP + i
                slot = (z - b + RING) % RING
                cum, mid, closing = running(gb[h, slot])
                qn = unit_rows(qb[h, slot].astype(F32))
                attend = dot3(split(qn * jnp.exp(cum - mid)), split(behind[h, b]), True)
                attend = jnp.where(row >= col, attend, 0.0)
                left = jnp.concatenate([qn * jnp.exp(cum), attend], 1)
                right = jnp.concatenate([entry[i], update[i]], 0)
                l, r = split(left), split(right)
                out = mm(l[0], r[0]) + (mm(l[0], r[1]) + mm(l[1], r[0]))
                ob[h, (b - z + RING) % RING] = out.astype(BF)
            return carry

        lax.fori_loop(0, RING // GROUP, group, 0)

    def to_sibling(j):
        return remote(
            spans.at[2 * j + 1 - core, RING], sib.at[j], scan_send.at[j, 0], scan_recv.at[j, 0], (peer, z)
        )

    def to_x(j, d):
        return remote(
            chip.at[j], xb.at[j, d], scan_send.at[j, 1 + d], scan_recv.at[j, 1 + d], (x_peers[d], z)
        )

    def to_y(j, d):
        return remote(
            yb.at[j, 3], yb.at[j, d], scan_send.at[j, 4 + d], scan_recv.at[j, 4 + d], (y_peers[d], z)
        )

    def to_enter(j):
        return remote(
            enter.at[j, 1], enter.at[j, 2], scan_send.at[j, 7], scan_recv.at[j, 7], (peer, z)
        )

    def over_chip(j):
        to_sibling(j).wait_recv()
        own, other = spans[2 * j + core, RING], sib[j]
        first[j] = jnp.where(core == 0, own, other)
        chip[j] = compose(jnp.where(core == 0, other, own), first[j])
        for d in range(3):
            to_x(j, d).start()

    def over_x(j):
        for d in range(3):
            to_x(j, d).wait_recv()
        place = []
        for i in range(4):
            far = (x - i + 4) % 4
            place.append(
                jnp.where(
                    far == 0,
                    chip[j],
                    jnp.where(far == 1, xb[j, 0], jnp.where(far == 2, xb[j, 1], xb[j, 2])),
                )
            )
        two = compose(place[1], place[0])
        yb[j, 3] = compose(compose(place[3], place[2]), two)
        for d in range(3):
            to_y(j, d).start()
        three = compose(place[2], two)
        before[j] = jnp.where(
            x == 0,
            spans[0, 0],
            jnp.where(x == 1, place[0], jnp.where(x == 2, two, three)),
        )

    def over_y(j):
        for d in range(3):
            to_y(j, d).wait_recv()
        place = []
        for i in range(3):
            far = (y - i + 4) % 4
            place.append(
                jnp.where(
                    far == 0,
                    yb[j, 3],
                    jnp.where(far == 1, yb[j, 0], jnp.where(far == 2, yb[j, 1], yb[j, 2])),
                )
            )
        one = place[0][:, DK:]
        two = advance(place[1], one)
        three = advance(place[2], two)
        state = jnp.where(y == 0, 0.0, jnp.where(y == 1, one, jnp.where(y == 2, two, three)))
        state = advance(before[j], state)
        after = advance(first[j], state)
        enter[j, 0] = jnp.where(core == 0, state, after)
        enter[j, 1] = jnp.where(core == 0, after, state)
        to_enter(j).start()

    def turn_in(h, carry):
        pl.when(h == 2)(lambda: over_chip(0))
        wait_in((0, 1, 2), h)
        maps(h)
        pl.when(h == 1)(lambda: to_sibling(0).start())
        pl.when(h == 2)(lambda: over_x(0))
        pl.when(h == 3)(lambda: to_sibling(1).start())
        return carry

    lax.fori_loop(0, HEADS, turn_in, 0)

    def turn_out(h, carry):
        @pl.when(h == 0)
        def _():
            over_y(0)
            over_chip(1)
            to_enter(0).wait_recv()

        pl.when(h == 1)(lambda: over_x(1))

        @pl.when(h == 2)
        def _():
            over_y(1)
            to_enter(1).wait_recv()

        wait_in((3,), h)
        j, half = h // 2, h % 2
        read_out(h, jnp.where(core == half, enter[j, 0], enter[j, 2]))
        own_out(h).start()
        over_peers(lambda d: outgoing(h, d).start())
        return carry

    lax.fori_loop(0, HEADS, turn_out, 0)

    def finish(h, carry):
        own_out(h).wait()
        over_peers(lambda d: outgoing(h, d).wait())
        for a in range(4):
            over_peers(lambda d: incoming(a, h, d).wait_send())
        return carry

    lax.fori_loop(0, HEADS, finish, 0)
    over_peers(lambda d: rates(d).wait_send())
    for j in range(2):
        to_sibling(j).wait_send()
        to_enter(j).wait_send()
        for d in range(3):
            to_x(j, d).wait_send()
            to_y(j, d).wait_send()


def local(query_rows, key_rows, value_rows, log_decay, write_rate):
    rows, heads = write_rate.shape
    anywhere = pl.BlockSpec(memory_space=pl.ANY)
    block = pltpu.VMEM((HEADS, RING, L, DK), BF)
    wide = pltpu.VMEM((HEADS, RING, L, DK), F32)
    pair = pltpu.VMEM((2, DK, 2 * DK), F32)
    return pl.pallas_call(
        kernel,
        in_specs=[anywhere] * 5,
        out_specs=anywhere,
        out_shape=jax.ShapeDtypeStruct(query_rows.shape, BF),
        scratch_shapes=[
            block,
            block,
            block,
            block,
            pltpu.VMEM((RING, rows, heads), BF),
            block,
            wide,
            wide,
            wide,
            pltpu.VMEM((HEADS, RING + 1, DK, 2 * DK), F32),
            pair,
            pair,
            pair,
            pltpu.VMEM((2, 3, DK, 2 * DK), F32),
            pair,
            pltpu.VMEM((2, 4, DK, 2 * DK), F32),
            pltpu.VMEM((2, 3, DK, DK), F32),
            pltpu.SemaphoreType.DMA((4, HEADS, RING)),
            pltpu.SemaphoreType.DMA((4, HEADS, RING)),
            pltpu.SemaphoreType.DMA((HEADS, RING)),
            pltpu.SemaphoreType.DMA((HEADS, RING)),
            pltpu.SemaphoreType.DMA((RING,)),
            pltpu.SemaphoreType.DMA((RING,)),
            pltpu.SemaphoreType.DMA((2, 8)),
            pltpu.SemaphoreType.DMA((2, 8)),
        ],
        compiler_params=pltpu.CompilerParams(
            vmem_limit_bytes=48 * 2**20, collective_id=0, has_side_effects=True
        ),
    )(query_rows, key_rows, value_rows, log_decay, write_rate)


def solution(mesh):
    spec = P(("seq", "head"), None)
    return jax.shard_map(
        local, mesh=mesh, in_specs=(spec,) * 5, out_specs=spec, check_vma=False
    )
```

time: 242 us -> 145 us (0.60)
  waiting for transfers between devices: 114 us -> 0 us
  Pallas kernels: 58.4 us -> 136 us
  blocking collectives: 31.7 us -> 0 us
  starting transfers between devices: 23.2 us -> 0 us
  local copies, waits for them, and re-layouts: 12.1 us -> 6.68 us
    all_to_all x5 -> x0, waiting for transfers between devices: 114 us -> none  [moved(): return lax.all_to_all(a, 'head', split_axis=1, concat_axis=0, tiled=True)]
    pallas_call x2 -> x1, Pallas kernels: 58.4 us -> 136 us  [local(): pl.pallas_call(kernel, in_specs=[anywhere] * 5, out_specs=anywhere, out_s...]
    all_to_all x1 -> x0, blocking collectives: 31.7 us -> none  [local(): return lax.all_to_all(out, 'head', split_axis=0, concat_axis=1, tiled=True)]
    all_to_all x5 -> x0, starting transfers between devices: 23.2 us -> none  [moved(): return lax.all_to_all(a, 'head', split_axis=1, concat_axis=0, tiled=True)]
    all_to_all x5 -> x0, local copies, waits for them, and re-layouts: 7.91 us -> none  [the longest x4 6.82 us: moved(): return lax.all_to_all(a, 'head', split_axis=1, concat_axis=0, tiled=True)]
    unnamed x6 -> x10, local copies, waits for them, and re-layouts: 2.19 us -> 6.68 us
  transfers between devices with their start and end apart: 5 -> 0, of which waited for: 5 -> 0; matrix products, arithmetic and copies ran while one was open for 4% -> 0% of each run, Pallas kernels for 0% -> 0%
where the time goes in v2:
time: 145 us; the launch traced here: 142 us
  Pallas kernels  136 us (94%)
  local copies, waits for them, and re-layouts  6.68 us (5%)
    pallas_call x1, Pallas kernels, local(): pl.pallas_call(kernel, in_specs=[anywhere] * 5, out_specs=anywhere, out_s...  136 us
    unnamed x10, local copies, waits for them, and re-layouts  6.68 us

profile of v2, /device:TPU:17, one launch (start us, length us, event | category | flops | bytes accessed | tf_op | source)
XLA Modules:
  0.0 142.3 jit_solution(11304880031620456731)
XLA Ops:
  0.0 0.8 copy.6.rate_ref
  0.8 0.0 copy-start
  0.8 1.2 copy-done
  2.0 0.0 copy-start.1
  2.0 1.2 copy-done.1
  3.3 0.0 copy-start.2
  3.3 1.2 copy-done.2
  4.5 0.0 copy-start.3
  4.5 1.2 copy-done.3
  5.7 135.6 %shard_map.55 = bf16[128,4096]{1,0:T(8,128)(2,1)S(1)} custom-call(bf16[128,4096]{1,0:T(8,128)(2,1)S(1)} %copy-done, bf16[128,4096]{1,0:T(8,128)(2,1)S(1)} %copy-done.1, bf16[128,4096]{1,0:T(8,128)(2,1)S(1)} %copy-done.2, bf16[128,4096]{1,0:T(8,128)(2,1)S(1)} %copy-done.3, bf16[128,32]{1,0:T(8,128)(2,1)S(1)} %copy.6.rate_ref), custom_call_target="tpu_custom_call" | custom-call | tf_op jit(solution)/shard_map/pallas_call | solution.py:391
  141.4 1.0 copy.8
Async XLA Ops:
  0.8 1.2 copy-start
  2.0 1.2 copy-start.1
  3.3 1.2 copy-start.2
  4.5 1.2 copy-start.3

commit v3 on v2

--- a/solution.py
+++ b/solution.py
@@ -10,6 +10,7 @@
 DK = 128
 L = 128
 RING = 8
+LIMIT = 52
 HEADS = 4
 GROUP = 4
 F32 = jnp.float32
@@ -86,7 +87,7 @@
 
 def kernel(
     q_ref, k_ref, v_ref, g_ref, rate_ref, out_ref,
-    kb, gb, vb, qb, rb, ob, inv, past, behind, spans,
+    kb, gb, vb, qb, rb, ob, inv, past, behind, weight, spans,
     sib, chip, first, xb, before, yb, enter,
     in_send, in_recv, out_send, out_recv, rate_send, rate_recv, scan_send, scan_recv,
 ):
@@ -181,21 +182,18 @@
 
     def maps(h):
         spans[h, 0] = jnp.concatenate([jnp.where(eye, 1.0, 0.0), jnp.zeros((L, DK), F32)], 1)
-        lane = lax.broadcasted_iota(jnp.int32, (L, rb.shape[2]), 1)
-        mine = lane == z * HEADS + h
+        mine = lax.broadcasted_iota(jnp.int32, rb.shape[1:], 0) == z * HEADS + h
 
         def group(n, carry):
             pre = []
             for i in range(GROUP):
                 b = n * GROUP + i
                 slot = (z - b + RING) % RING
-                rate = jnp.sum(
-                    jnp.where(mine, rb[slot].astype(F32), 0.0), axis=1, keepdims=True
-                )
+                rate = jnp.sum(jnp.where(mine, rb[slot].astype(F32), 0.0), axis=0, keepdims=True)
+                weight[h, b] = rate
                 cum, mid, closing = running(gb[h, slot])
                 kn = unit_rows(kb[h, slot].astype(F32))
-                kr = kn * rate
-                back = kr * jnp.exp(mid - cum)
+                back = kn * jnp.exp(mid - cum)
                 kp = kn * jnp.exp(cum)
                 behind[h, b] = back
                 past[h, b] = kp
@@ -204,12 +202,13 @@
                         split(kn * jnp.exp(cum - mid)),
                         split(back),
                         split(kp),
-                        split((kr * jnp.exp(closing - cum)).T),
+                        split((kn * jnp.exp(closing - cum)).T * rate),
                         jnp.where(eye, jnp.exp(closing), 0.0),
                         vb[h, slot],
+                        rate,
                     )
                 )
-            among = [jnp.where(row > col, dot3(p[0], p[1], True), 0.0) for p in pre]
+            among = [jnp.where(row > col, dot3(p[0], p[1], True), 0.0) * p[6] for p in pre]
             inverse = unit_inverse(among)
             steps = []
             for i in range(GROUP):
@@ -246,12 +245,16 @@
                 cum, mid, closing = running(gb[h, slot])
                 qn = unit_rows(qb[h, slot].astype(F32))
                 attend = dot3(split(qn * jnp.exp(cum - mid)), split(behind[h, b]), True)
-                attend = jnp.where(row >= col, attend, 0.0)
+                attend = jnp.where(row >= col, attend, 0.0) * weight[h, b]
                 left = jnp.concatenate([qn * jnp.exp(cum), attend], 1)
                 right = jnp.concatenate([entry[i], update[i]], 0)
                 l, r = split(left), split(right)
                 out = mm(l[0], r[0]) + (mm(l[0], r[1]) + mm(l[1], r[0]))
                 ob[h, (b - z + RING) % RING] = out.astype(BF)
+            for i in range(GROUP):
+                d = (n * GROUP + i - z + RING) % RING
+                pl.when(d == 0)(lambda: own_out(h).start())
+                pl.when(d != 0)(lambda d=d: outgoing(h, d).start())
             return carry
 
         lax.fori_loop(0, RING // GROUP, group, 0)
@@ -359,8 +362,6 @@
         wait_in((3,), h)
         j, half = h // 2, h % 2
         read_out(h, jnp.where(core == half, enter[j, 0], enter[j, 2]))
-        own_out(h).start()
-        over_peers(lambda d: outgoing(h, d).start())
         return carry
 
     lax.fori_loop(0, HEADS, turn_out, 0)
@@ -384,25 +385,26 @@
 
 def local(query_rows, key_rows, value_rows, log_decay, write_rate):
     rows, heads = write_rate.shape
-    anywhere = pl.BlockSpec(memory_space=pl.ANY)
+    anywhere = pl.BlockSpec(memory_space=pltpu.HBM)
     block = pltpu.VMEM((HEADS, RING, L, DK), BF)
     wide = pltpu.VMEM((HEADS, RING, L, DK), F32)
     pair = pltpu.VMEM((2, DK, 2 * DK), F32)
     return pl.pallas_call(
         kernel,
         in_specs=[anywhere] * 5,
-        out_specs=anywhere,
+        out_specs=pl.BlockSpec(memory_space=pltpu.VMEM),
         out_shape=jax.ShapeDtypeStruct(query_rows.shape, BF),
         scratch_shapes=[
             block,
             block,
             block,
             block,
-            pltpu.VMEM((RING, rows, heads), BF),
+            pltpu.VMEM((RING, heads, rows), BF),
             block,
             wide,
             wide,
             wide,
+            pltpu.VMEM((HEADS, RING, 1, L), F32),
             pltpu.VMEM((HEADS, RING + 1, DK, 2 * DK), F32),
             pair,
             pair,
@@ -421,9 +423,9 @@
             pltpu.SemaphoreType.DMA((2, 8)),
         ],
         compiler_params=pltpu.CompilerParams(
-            vmem_limit_bytes=48 * 2**20, collective_id=0, has_side_effects=True
+            vmem_limit_bytes=LIMIT * 2**20, collective_id=0, has_side_effects=True
         ),
-    )(query_rows, key_rows, value_rows, log_decay, write_rate)
+    )(query_rows, key_rows, value_rows, log_decay, write_rate.T)
 
 
 def solution(mesh):

time: 145 us -> 133 us (0.917)
  Pallas kernels: 136 us -> 129 us
  local copies, waits for them, and re-layouts: 6.68 us -> 1.67 us
    pallas_call x1, Pallas kernels: 136 us -> 129 us  [local(): pl.pallas_call(kernel, in_specs=[anywhere] * 5, out_specs=pl.BlockSpec(me...]
    unnamed x10 -> x3, local copies, waits for them, and re-layouts: 6.68 us -> 1.67 us
where the time goes in v3:
time: 133 us; the launch traced here: 131 us
  Pallas kernels  129 us (97%)
  local copies, waits for them, and re-layouts  1.67 us (1%)
    pallas_call x1, Pallas kernels, local(): pl.pallas_call(kernel, in_specs=[anywhere] * 5, out_specs=pl.BlockSpec(me...  129 us

profile of v3, /device:TPU:17, one launch (start us, length us, event | category | flops | bytes accessed | tf_op | source)
XLA Modules:
  0.0 130.9 jit_solution(12309064154786877455)
XLA Ops:
  0.0 0.0 copy-start
  0.0 0.7 copy-done
  0.7 129.2 %shard_map.55 = bf16[128,4096]{1,0:T(8,128)(2,1)S(1)} custom-call(bf16[128,4096]{1,0:T(8,128)(2,1)} %q_ref.1, bf16[128,4096]{1,0:T(8,128)(2,1)} %k_ref.1, bf16[128,4096]{1,0:T(8,128)(2,1)} %v_ref.1, bf16[128,4096]{1,0:T(8,128)(2,1)} %g_ref.1, bf16[32,128]{1,0:T(8,128)(2,1)S(1)} %bitcast.1), custom_call_target="tpu_custom_call" | custom-call | tf_op jit(solution)/shard_map/pallas_call | solution.py:392
  129.9 1.0 copy.7
Async XLA Ops:
  0.0 0.7 copy-start

commit v4 on v3

--- a/solution.py
+++ b/solution.py
@@ -186,8 +186,8 @@
 
         def group(n, carry):
             pre = []
-            for i in range(GROUP):
-                b = n * GROUP + i
+            for i in range(RING):
+                b = n * RING + i
                 slot = (z - b + RING) % RING
                 rate = jnp.sum(jnp.where(mine, rb[slot].astype(F32), 0.0), axis=0, keepdims=True)
                 weight[h, b] = rate
@@ -211,17 +211,17 @@
             among = [jnp.where(row > col, dot3(p[0], p[1], True), 0.0) * p[6] for p in pre]
             inverse = unit_inverse(among)
             steps = []
-            for i in range(GROUP):
-                inv[h, n * GROUP + i] = inverse[i]
+            for i in range(RING):
+                inv[h, n * RING + i] = inverse[i]
                 reach = split(dot3(pre[i][3], split(inverse[i])))
                 steps.append((pre[i][4] - dot3(reach, pre[i][2]), dot2(reach, pre[i][5])))
-            prefix = spans[h, n * GROUP]
-            for i in range(GROUP):
+            prefix = spans[h, n * RING]
+            for i in range(RING):
                 prefix = compose(jnp.concatenate(steps[i], 1), prefix)
-                spans[h, n * GROUP + i + 1] = prefix
+                spans[h, n * RING + i + 1] = prefix
             return carry
 
-        lax.fori_loop(0, RING // GROUP, group, 0)
+        group(0, 0)
 
     def read_out(h, state):
         halves = split(state)
@@ -274,6 +274,13 @@
             yb.at[j, 3], yb.at[j, d], scan_send.at[j, 4 + d], scan_recv.at[j, 4 + d], (y_peers[d], z)
         )
 
+    def on_y(j, start):
+        for d in range(3):
+            if start:
+                pl.when(y + d + 1 < 4)(lambda d=d: to_y(j, d).start())
+            else:
+                pl.when(y >= d + 1)(lambda d=d: to_y(j, d).wait_recv())
+
     def to_enter(j):
         return remote(
             enter.at[j, 1], enter.at[j, 2], scan_send.at[j, 7], scan_recv.at[j, 7], (peer, z)
@@ -302,8 +309,7 @@
             )
         two = compose(place[1], place[0])
         yb[j, 3] = compose(compose(place[3], place[2]), two)
-        for d in range(3):
-            to_y(j, d).start()
+        on_y(j, True)
         three = compose(place[2], two)
         before[j] = jnp.where(
             x == 0,
@@ -312,8 +318,7 @@
         )
 
     def over_y(j):
-        for d in range(3):
-            to_y(j, d).wait_recv()
+        on_y(j, False)
         place = []
         for i in range(3):
             far = (y - i + 4) % 4
@@ -380,7 +385,7 @@
         to_enter(j).wait_send()
         for d in range(3):
             to_x(j, d).wait_send()
-            to_y(j, d).wait_send()
+            pl.when(y + d + 1 < 4)(lambda d=d: to_y(j, d).wait_send())
 
 
 def local(query_rows, key_rows, value_rows, log_decay, write_rate):

time: 133 us -> 129 us (0.970); the launches traced: 131 us -> 129 us
  Pallas kernels: 129 us -> 127 us
    pallas_call x1, Pallas kernels: 129 us -> 127 us  [local(): pl.pallas_call(kernel, in_specs=[anywhere] * 5, out_specs=pl.BlockSpec(me...]
where the time goes in v4:
time: 129 us
  Pallas kernels  127 us (98%)
  local copies, waits for them, and re-layouts  1.67 us (1%)
    pallas_call x1, Pallas kernels, local(): pl.pallas_call(kernel, in_specs=[anywhere] * 5, out_specs=pl.BlockSpec(me...  127 us

profile of v4, /device:TPU:17, one launch (start us, length us, event | category | flops | bytes accessed | tf_op | source)
XLA Modules:
  0.0 128.8 jit_solution(9694482485536665519)
XLA Ops:
  0.0 0.0 copy-start
  0.0 0.7 copy-done
  0.7 127.1 %shard_map.55 = bf16[128,4096]{1,0:T(8,128)(2,1)S(1)} custom-call(bf16[128,4096]{1,0:T(8,128)(2,1)} %q_ref.1, bf16[128,4096]{1,0:T(8,128)(2,1)} %k_ref.1, bf16[128,4096]{1,0:T(8,128)(2,1)} %v_ref.1, bf16[128,4096]{1,0:T(8,128)(2,1)} %g_ref.1, bf16[32,128]{1,0:T(8,128)(2,1)S(1)} %bitcast.1), custom_call_target="tpu_custom_call" | custom-call | tf_op jit(solution)/shard_map/pallas_call | solution.py:397
  127.8 1.0 copy.7
Async XLA Ops:
  0.0 0.7 copy-start

commit v5 on v4

--- a/solution.py
+++ b/solution.py
@@ -28,10 +28,15 @@
 
 
 def dot3(a, b, turned=False):
-    dims = ((1,), (1,)) if turned else ((1,), (0,))
     wide = jnp.concatenate([a[0], a[1]], 1)
-    twice = jnp.concatenate([b[0], b[0]], 1 if turned else 0)
-    return mm(wide, twice, dims) + mm(a[0], b[1], dims)
+    if turned:
+        both = jnp.concatenate([b[0], b[1]], 0)
+        product = mm(wide, jnp.concatenate([both, both], 1), ((1,), (1,)))
+    else:
+        both = jnp.concatenate([b[0], b[1]], 1)
+        product = mm(wide, jnp.concatenate([both, both], 0))
+    half = product.shape[1] // 2
+    return product[:, :half] + product[:, half:]
 
 
 def dot2(a, b):
@@ -132,9 +137,12 @@
         src, dst = arrays[a]
         return pltpu.make_async_copy(src.at[:, columns(z, h)], dst.at[h, 0], in_recv.at[a, h, 0])
 
+    def rate_part(owner):
+        return rate_ref.at[pl.ds(pl.multiple_of(owner // 4 * 16, 16), 16), :]
+
     def rates(d):
         to = (z + d) % RING
-        return remote(rate_ref, rb.at[d], rate_send.at[d], rate_recv.at[d], (me, to))
+        return remote(rate_part(to), rb.at[d], rate_send.at[d], rate_recv.at[d], (me, to))
 
     def outgoing(h, d):
         to = (z + d) % RING
@@ -145,7 +153,7 @@
     def own_out(h):
         return pltpu.make_async_copy(ob.at[h, 0], out_ref.at[:, columns(z, h)], out_recv.at[h, 0])
 
-    own_rate = pltpu.make_async_copy(rate_ref, rb.at[0], rate_recv.at[0])
+    own_rate = pltpu.make_async_copy(rate_part(z), rb.at[0], rate_recv.at[0])
 
     def over_peers(act):
         def one(d, carry):
@@ -182,7 +190,7 @@
 
     def maps(h):
         spans[h, 0] = jnp.concatenate([jnp.where(eye, 1.0, 0.0), jnp.zeros((L, DK), F32)], 1)
-        mine = lax.broadcasted_iota(jnp.int32, rb.shape[1:], 0) == z * HEADS + h
+        mine = lax.broadcasted_iota(jnp.int32, rb.shape[1:], 0) == z % 4 * HEADS + h
 
         def group(n, carry):
             pre = []
@@ -371,14 +379,12 @@
 
     lax.fori_loop(0, HEADS, turn_out, 0)
 
-    def finish(h, carry):
-        own_out(h).wait()
-        over_peers(lambda d: outgoing(h, d).wait())
+    def sent(h, carry):
         for a in range(4):
             over_peers(lambda d: incoming(a, h, d).wait_send())
         return carry
 
-    lax.fori_loop(0, HEADS, finish, 0)
+    lax.fori_loop(0, HEADS, sent, 0)
     over_peers(lambda d: rates(d).wait_send())
     for j in range(2):
         to_sibling(j).wait_send()
@@ -387,9 +393,16 @@
             to_x(j, d).wait_send()
             pl.when(y + d + 1 < 4)(lambda d=d: to_y(j, d).wait_send())
 
+    def finish(h, carry):
+        own_out(h).wait()
+        over_peers(lambda d: outgoing(h, d).wait())
+        return carry
+
+    lax.fori_loop(0, HEADS, finish, 0)
+
 
 def local(query_rows, key_rows, value_rows, log_decay, write_rate):
-    rows, heads = write_rate.shape
+    rows = write_rate.shape[0]
     anywhere = pl.BlockSpec(memory_space=pltpu.HBM)
     block = pltpu.VMEM((HEADS, RING, L, DK), BF)
     wide = pltpu.VMEM((HEADS, RING, L, DK), F32)
@@ -404,7 +417,7 @@
             block,
             block,
             block,
-            pltpu.VMEM((RING, heads, rows), BF),
+            pltpu.VMEM((RING, 16, rows), BF),
             block,
             wide,
             wide,

time: 129 us -> 128 us (level)
    pallas_call x1, Pallas kernels: 127 us -> 126 us  [local(): pl.pallas_call(kernel, in_specs=[anywhere] * 5, out_specs=pl.BlockSpec(me...]
where the time goes in v5:
time: 128 us; the launch traced here: 127 us
  Pallas kernels  126 us (98%)
  local copies, waits for them, and re-layouts  1.67 us (1%)
    pallas_call x1, Pallas kernels, local(): pl.pallas_call(kernel, in_specs=[anywhere] * 5, out_specs=pl.BlockSpec(me...  126 us

profile of v5, /device:TPU:17, one launch (start us, length us, event | category | flops | bytes accessed | tf_op | source)
XLA Modules:
  0.0 127.4 jit_solution(17736009287026595808)
XLA Ops:
  0.0 0.0 copy-start
  0.0 0.7 copy-done
  0.7 125.7 %shard_map.55 = bf16[128,4096]{1,0:T(8,128)(2,1)S(1)} custom-call(bf16[128,4096]{1,0:T(8,128)(2,1)} %q_ref.1, bf16[128,4096]{1,0:T(8,128)(2,1)} %k_ref.1, bf16[128,4096]{1,0:T(8,128)(2,1)} %v_ref.1, bf16[128,4096]{1,0:T(8,128)(2,1)} %g_ref.1, bf16[32,128]{1,0:T(8,128)(2,1)S(1)} %bitcast.1), custom_call_target="tpu_custom_call" | custom-call | tf_op jit(solution)/shard_map/pallas_call | solution.py:410
  126.4 1.0 copy.7
Async XLA Ops:
  0.0 0.7 copy-start

commit v6 on v5

--- a/solution.py
+++ b/solution.py
@@ -105,17 +105,6 @@
     row, col = masks()
     eye = row == col
 
-    barrier = pltpu.get_barrier_semaphore()
-
-    def greet(d, carry):
-        pl.semaphore_signal(barrier, inc=1, device_id=(me, (z + d) % RING), device_id_type=MESH)
-        return carry
-
-    lax.fori_loop(1, RING, greet, 0)
-    for to in [peer] + x_peers + y_peers:
-        pl.semaphore_signal(barrier, inc=1, device_id=(to, z), device_id_type=MESH)
-    pl.semaphore_wait(barrier, RING + 6)
-
     def columns(owner, h):
         return pl.ds(pl.multiple_of((owner * HEADS + h) * DK, DK), DK)
 
@@ -164,7 +153,6 @@
 
     def start_in(which, h):
         for a in which:
-            own_block(a, h).start()
             over_peers(lambda d: incoming(a, h, d).start())
 
     def wait_in(which, h):
@@ -172,8 +160,6 @@
             own_block(a, h).wait()
             over_peers(lambda d: incoming(a, h, d).wait_recv())
 
-    own_rate.start()
-    over_peers(lambda d: rates(d).start())
 
     def send_three(h, carry):
         start_in((0, 1, 2), h)
@@ -183,7 +169,28 @@
         start_in((3,), h)
         return carry
 
-    lax.fori_loop(0, HEADS, send_three, 0)
+    own_rate.start()
+
+    def keep_own(h, carry):
+        for a in range(4):
+            own_block(a, h).start()
+        return carry
+
+    barrier = pltpu.get_barrier_semaphore()
+
+    def greet(d, carry):
+        pl.semaphore_signal(barrier, inc=1, device_id=(me, (z + d) % RING), device_id_type=MESH)
+        return carry
+
+    for to in [peer] + x_peers + y_peers:
+        pl.semaphore_signal(barrier, inc=1, device_id=(to, z), device_id_type=MESH)
+    lax.fori_loop(1, RING, greet, 0)
+    lax.fori_loop(0, HEADS, keep_own, 0)
+    pl.semaphore_wait(barrier, RING + 6)
+
+    send_three(0, 0)
+    over_peers(lambda d: rates(d).start())
+    lax.fori_loop(1, HEADS, send_three, 0)
     lax.fori_loop(0, HEADS, send_query, 0)
     own_rate.wait()
     over_peers(lambda d: rates(d).wait_recv())

time: 128 us -> 128 us (level)
  no operation moved by 1% of the time
where the time goes in v6:
time: 128 us
  Pallas kernels  126 us (98%)
  local copies, waits for them, and re-layouts  1.67 us (1%)
    pallas_call x1, Pallas kernels, local(): pl.pallas_call(kernel, in_specs=[anywhere] * 5, out_specs=pl.BlockSpec(me...  126 us

profile of v6, /device:TPU:17, one launch (start us, length us, event | category | flops | bytes accessed | tf_op | source)
XLA Modules:
  0.0 127.9 jit_solution(9079255238928546175)
XLA Ops:
  0.0 0.0 copy-start
  0.0 0.7 copy-done
  0.7 126.2 %shard_map.55 = bf16[128,4096]{1,0:T(8,128)(2,1)S(1)} custom-call(bf16[128,4096]{1,0:T(8,128)(2,1)} %q_ref.1, bf16[128,4096]{1,0:T(8,128)(2,1)} %k_ref.1, bf16[128,4096]{1,0:T(8,128)(2,1)} %v_ref.1, bf16[128,4096]{1,0:T(8,128)(2,1)} %g_ref.1, bf16[32,128]{1,0:T(8,128)(2,1)S(1)} %bitcast.1), custom_call_target="tpu_custom_call" | custom-call | tf_op jit(solution)/shard_map/pallas_call | solution.py:417
  126.9 1.0 copy.7
Async XLA Ops:
  0.0 0.7 copy-start
